TPU v7x, 1024 devices: a whole 8x8x8 slice. The times are simulated.
1024 devices in a mesh: shot: 16 (over y_lo, x), dom: 64 (over z, y_hi, core).
Axes of the slice: x: 8, y: 8 (y_hi: 4, y_lo: 2; y = y_hi * 2 + y_lo), z: 8, core: 2. Of those that a mesh axis runs over, the one named last changes fastest.
Arguments:
- stiffness: float32 [512, 64, 128], P('dom'), may hold values from 0.04 to 0.16
- buoyancy: float32 [512, 64, 128], P('dom'), may hold values from 0.6 to 1.2
- forward_now: float32 [16, 512, 64, 128], P('shot', 'dom'), may hold values from -3 to 3
- forward_prior: float32 [16, 512, 64, 128], P('shot', 'dom'), may hold values from -3 to 3
- adjoint_now: float32 [16, 512, 64, 128], P('shot', 'dom'), may hold values from -3 to 3
- adjoint_after: float32 [16, 512, 64, 128], P('shot', 'dom'), may hold values from -3 to 3
- source_cells: int32 [16], P('shot'), may hold values from 0 to 4194303
- wavelet: float32 [16, 1], P('shot'), may hold values from -500 to 500
- receiver_cells: int32 [16, 256], P('shot'), may hold values from 0 to 4194303
- residuals: float32 [16, 2, 256], P('shot'), may hold values from -60 to 60
Outputs:
- gradient: float32 [512, 64, 128], P('dom')
Inputs may be any that keep to these rules, and one draw needn't show every extreme that they name: `source_cells`: a flat cell index of the grid. `receiver_cells`: flat cell indices of the grid; a cell may repeat.
All inputs are finite; a program needn't handle non-finite values.
Results may differ from a plain program's by a relative error of at most 0.0003.
Values sent between devices are 32-bit elements; how exact they have to be, the bound alone decides.
A program may use at most 64 MiB of HBM per device.

v0:
```python
import jax
import jax.numpy as jnp
from jax import lax
from jax.sharding import PartitionSpec as P

C_SECOND = (-205.0 / 72.0, 8.0 / 5.0, -1.0 / 5.0, 8.0 / 315.0, -1.0 / 560.0)
C_FIRST = (4.0 / 5.0, -1.0 / 5.0, 4.0 / 105.0, -1.0 / 280.0)


def padded_2(x, sides, width):
    for axis, dim in sides:
        size, length = (lax.axis_size(axis), x.shape[dim])
        up = [(i, (i + 1) % size) for i in range(size - 1)]
        down = [(j, i) for i, j in up]
        last = lax.slice_in_dim(x, length - width, length, axis=dim)
        first = lax.slice_in_dim(x, 0, width, axis=dim)
        before = lax.ppermute(last, axis, up)
        after = lax.ppermute(first, axis, down)
        x = jnp.concatenate([before, x, after], axis=dim)
    return x


def window(padded, dimension, shift):
    depth = padded.shape[0] - 8
    width_x = padded.shape[1] - 8
    width_y = padded.shape[2] - 8
    starts = [4, 4, 4]
    starts[dimension] = starts[dimension] + shift
    return padded[
        starts[0] : starts[0] + depth,
        starts[1] : starts[1] + width_x,
        starts[2] : starts[2] + width_y,
    ]


def operate(field, buoy_pad):
    field_pad = jnp.pad(field, ((0, 0), (4, 4), (4, 4)))
    curvature = 3.0 * C_SECOND[0] * window(field_pad, 0, 0)
    products = jnp.zeros_like(curvature)
    for dimension in range(3):
        slope_field = jnp.zeros_like(curvature)
        slope_buoy = jnp.zeros_like(curvature)
        for offset in range(1, 5):
            curvature = curvature + C_SECOND[offset] * (
                window(field_pad, dimension, offset) + window(field_pad, dimension, -offset)
            )
            slope_field = slope_field + C_FIRST[offset - 1] * (
                window(field_pad, dimension, offset) - window(field_pad, dimension, -offset)
            )
            slope_buoy = slope_buoy + C_FIRST[offset - 1] * (
                window(buoy_pad, dimension, offset) - window(buoy_pad, dimension, -offset)
            )
        products = products + slope_field * slope_buoy
    return window(buoy_pad, 0, 0) * curvature + products


def inject(field, first_plane, cells, amounts):
    depth = field.shape[0]
    plane_size = field.shape[1] * field.shape[2]
    local_cells = cells - first_plane * plane_size
    inside = (local_cells >= 0) & (local_cells < depth * plane_size)
    local_cells = jnp.where(inside, local_cells, depth * plane_size)
    flat = field.reshape(-1).at[local_cells].add(amounts, mode="drop")
    return flat.reshape(field.shape)


def edge_fix(extended, width):
    position = lax.axis_index("dom")
    count = lax.axis_size("dom")
    lower = extended[:width]
    upper = extended[extended.shape[0] - width :]
    low_edge = jnp.broadcast_to(extended[width : width + 1], lower.shape)
    high_edge = jnp.broadcast_to(
        extended[extended.shape[0] - width - 1 : extended.shape[0] - width], upper.shape
    )
    lower = jnp.where(position == 0, low_edge, lower)
    upper = jnp.where(position == count - 1, high_edge, upper)
    whole = jnp.concatenate([lower, extended[width : extended.shape[0] - width], upper], axis=0)
    return jnp.pad(whole, ((0, 0), (4, 4), (4, 4)), mode="edge")


def shards(
    stiffness,
    buoyancy,
    forward_now,
    forward_prior,
    adjoint_now,
    adjoint_after,
    source_cells,
    wavelet,
    receiver_cells,
    residuals,
):
    field = forward_now[0]
    earlier = forward_prior[0]
    adjoint = adjoint_now[0]
    after = adjoint_after[0]
    amplitudes = wavelet[0]
    receivers = receiver_cells[0]
    traces = residuals[0]
    steps = traces.shape[0]
    depth = field.shape[0]
    first_plane = lax.axis_index("dom") * depth
    images = []
    gradient = jnp.zeros_like(stiffness)

    def forward_single(padded, buoy_ext, field, earlier, step):
        image = operate(padded, buoy_ext)
        if step + 1 < steps:
            advanced = 2.0 * field - earlier + stiffness * image
            advanced = inject(advanced, first_plane, source_cells, amplitudes)
            return (image, advanced, field)
        return (image, field, earlier)

    buoy_ext = edge_fix(padded_2(buoyancy, (("dom", 0),), 4), 4)
    for step in range(steps):
        padded = padded_2(field, (("dom", 0),), 4)
        image, field, earlier = forward_single(padded, buoy_ext, field, earlier, step)
        images.append(image)
    for step in range(steps):
        padded = padded_2(stiffness * adjoint, (("dom", 0),), 4)
        retreated = 2.0 * adjoint - after + operate(padded, buoy_ext)
        retreated = inject(retreated, first_plane, receivers, traces[step])
        adjoint, after = (retreated, adjoint)
        gradient = gradient + adjoint * images[steps - 1 - step]
    return lax.psum(gradient, "shot")


def solution(mesh):
    placed = (
        P("dom", None, None),
        P("dom", None, None),
        P("shot", "dom", None, None),
        P("shot", "dom", None, None),
        P("shot", "dom", None, None),
        P("shot", "dom", None, None),
        P("shot"),
        P("shot", None),
        P("shot", None),
        P("shot", None, None),
    )
    return jax.shard_map(
        shards, mesh=mesh, in_specs=placed, out_specs=P("dom", None, None), check_vma=False
    )
```

profile of v0, /device:TPU:32, one launch (start us, length us, event | category | flops | bytes accessed | tf_op | source)
XLA Modules:
  0.0 252.4 jit_solution(13522545322788836772)
XLA Ops:
  6.5 1.2 copy.35
  7.8 1.9 collective-permute-start.2
  9.7 0.0 copy-start
  9.7 0.0 copy-start.27
  9.7 2.5 %collective-permute-start.3 = (f32[4,64,128]{2,0,1:T(4,128)S(1)}, f32[4,64,128]{2,0,1:T(4,128)S(1)}, u32[]{:S(2)}, u32[]{:S(2)}) collective-permute-start(f32[4,64,128]{2,0,1:T(4,128)S(1)} %get-tuple-element.41), channel_id=1, source_target_pairs={{0,1},{1,2},{2,3},{3,4},{4,5},{5,6},{6,7},{7,8},{8,9},{9,10},{10,1... | collective-permute-start | bytes 393224 | tf_op jit(solution)/shard_map/ppermute | solution.py:17
  12.3 0.2 copy.94
  12.5 0.7 slice_bitcast_fusion
  13.2 14.3 %collective-permute-start.4 = (f32[4,64,128]{2,0,1:T(4,128)}, f32[4,64,128]{2,0,1:T(4,128)S(1)}, u32[]{:S(2)}, u32[]{:S(2)}) collective-permute-start(f32[4,64,128]{2,0,1:T(4,128)} %get-tuple-element.36), channel_id=1, source_target_pairs={{1,0},{2,1},{3,2},{4,3},{5,4},{6,5},{7,6},{8,7},{9,8},{10,9},{11,1... | collective-permute-start | bytes 393224 | tf_op jit(solution)/shard_map/ppermute | solution.py:18
  27.5 1.9 collective-permute-start.5
  29.4 0.3 bitcast_multiply_fusion
  29.7 0.7 fusion.67
  30.5 4.5 %collective-permute-start = (f32[4,64,128]{2,0,1:T(4,128)}, f32[4,64,128]{2,0,1:T(4,128)S(1)}, u32[]{:S(2)}, u32[]{:S(2)}) collective-permute-start(f32[4,64,128]{2,0,1:T(4,128)} %get-tuple-element.34), channel_id=1, source_target_pairs={{1,0},{2,1},{3,2},{4,3},{5,4},{6,5},{7,6},{8,7},{9,8},{10,9},{11,1... | collective-permute-start | bytes 393224 | tf_op jit(solution)/shard_map/ppermute | solution.py:18
  37.0 1.9 collective-permute-start.1
  39.1 0.1 pad_maximum_fusion
  39.2 1.0 fusion.64
  40.1 1.5 copy.69
  41.7 0.5 copy.68
  42.2 2.3 collective-permute-done.1
  44.5 0.6 select_maximum_fusion.6
  45.1 0.1 pad_maximum_fusion.1
  45.3 0.6 select_maximum_fusion.4
  46.0 0.2 reshape.125
  46.2 0.2 reshape.124
  46.5 0.1 copy-done.26
  46.5 6.1 %fusion.56 = (f32[8,64,128]{2,0,1:T(8,128)}, f32[8,64,128]{2,0,1:T(8,128)}, f32[8,64,128]{2,0,1:T(8,128)S(1)}, f32[8,64,128]{2,0,1:T(8,128)S(1)}) fusion(f32[1,8,64,128]{3,2,1,0:T(8,128)S(1)} %copy-done.26, f32[8,64,128]{2,1,0:T(8,128)S(1)} %copy-done.5, f32[1,8,64,128]{3,2,1,0:T(8,128)S(1)} %copy-done.17, f32[16,4,128]{2,0,1:T(8,128)S(1)} %copy-done.8, ...), kind=kLoop, calls=%fused_computation.154 | loop fusion | flops 11141120 | bytes 9539584 | tf_op jit(solution)/shard_map/add | solution.py:110
  52.7 3.2 %fusion.57 = f32[8,64,128]{2,0,1:T(8,128)S(1)} fusion(f32[1,8,64,128]{3,2,1,0:T(8,128)S(1)} %copy-done.25, f32[8,64,128]{2,0,1:T(8,128)S(1)} %get-tuple-element.20, f32[8,64,128]{2,0,1:T(8,128)S(1)} %get-tuple-element.19, f32[16,72,136]{2,0,1:T(8,128)S(1)} %select_maximum_fusion.6, f32[4,64,128]{2,0,1:T(4,128)S(1)} %copy-done.20, ...), kind=kLoop, calls=%fused_computation.156 | loop fusion | flops 9109504 | bytes 6918144 | tf_op jit(solution)/shard_map/add | solution.py:122
  55.9 0.1 copy.45
  56.0 2.1 scatter_fusion
  58.1 0.3 copy_multiply_fusion.1
  58.4 2.3 collective-permute-start.8
  60.7 2.0 collective-permute-start.9
  62.8 0.1 copy.52
  62.8 1.6 fusion.61
  64.4 0.7 copy.54
  65.2 4.4 %collective-permute-start.6 = (f32[4,64,128]{2,0,1:T(4,128)}, f32[4,64,128]{2,0,1:T(4,128)}, u32[]{:S(2)}, u32[]{:S(2)}) collective-permute-start(f32[4,64,128]{2,0,1:T(4,128)} %copy.54), channel_id=1, source_target_pairs={{1,0},{2,1},{3,2},{4,3},{5,4},{6,5},{7,6},{8,7},{9,8},{10,9},{11,1... | collective-permute-start | bytes 393224 | tf_op jit(solution)/shard_map/ppermute | solution.py:18
  69.6 0.7 copy.56
  70.3 2.1 collective-permute-start.7
  72.4 0.9 constant_dynamic-update-slice_fusion.1
  73.3 0.6 select_maximum_fusion
  74.0 3.2 %fusion.58 = f32[8,64,128]{2,0,1:T(8,128)S(1)} fusion(f32[8,64,128]{2,0,1:T(8,128)S(1)} %get-tuple-element.20, f32[8,64,128]{2,0,1:T(8,128)S(1)} %get-tuple-element.19, f32[16,72,136]{2,0,1:T(8,128)S(1)} %select_maximum_fusion, f32[4,64,128]{2,0,1:T(4,128)S(1)} %collective-permute-done.8, f32[8,64,128]{2,0,1:T(8,128)S(1)} %copy_multiply_fusion.1, ...), kind=kLoop, calls=%fused_computation.160 | loop fusion | flops 9109504 | bytes 6918144 | tf_op jit(solution)/shard_map/add | solution.py:122
  77.2 0.1 copy.65
  77.2 2.1 scatter_fusion.1
  79.3 1.0 constant_dynamic-update-slice_fusion
  80.3 1.7 select_maximum_fusion.2
  82.1 4.9 %fusion.59 = f32[8,64,128]{2,0,1:T(8,128)} fusion(f32[8,64,128]{2,0,1:T(8,128)S(1)} %copy-done.15, f32[8,64,128]{2,1,0:T(8,128)S(1)} %bitcast.58, f32[8,64,128]{2,0,1:T(8,128)S(1)} %get-tuple-element.20, f32[8,64,128]{2,0,1:T(8,128)S(1)} %get-tuple-element.19, f32[16,72,136]{2,0,1:T(8,128)S(1)} %select_maximum_fusion.2, f32[8,64,128]{2,0,1:T(8,128)S(1)} %copy-done.3, ...), kind=kLoop, calls=%fused_computation.162 | loop fusion | flops 8847360 | bytes 8097792 | tf_op jit(solution)/shard_map/add | solution.py:125
  86.9 0.0 all-reduce.6.cloned.1.call-update
  87.0 156.9 %all-reduce.6.cloned.1.call-done = f32[8,64,128]{2,0,1:T(8,128)} async-done(((f32[8,64,128]{2,0,1:T(8,128)}), f32[8,64,128]{2,0,1:T(8,128)}) %all-reduce.6.cloned.1.call-update) | async-done | bytes 262160 | tf_op jit(solution)/shard_map/psum | solution.py:126
  243.8 1.7 copy.67
  (76 shorter events, 0.4 us)
Async XLA Ops:
  6.5 5.8 %copy-start.16 = (f32[1,8,64,128]{3,2,1,0:T(8,128)S(1)}, f32[1,8,64,128]{3,2,1,0:T(8,128)}, u32[]{:S(2)}) copy-start(f32[1,8,64,128]{3,2,1,0:T(8,128)} %param.14) | copy-start | bytes 786436
  6.5 22.9 %copy-start.4 = (f32[8,64,128]{2,1,0:T(8,128)S(1)}, f32[8,64,128]{2,1,0:T(8,128)}, u32[]{:S(2)}) copy-start(f32[8,64,128]{2,1,0:T(8,128)} %param.12) | copy-start | bytes 786436
  6.5 22.9 %copy-start.1 = (f32[1,8,64,128]{3,2,1,0:T(8,128)S(1)}, f32[1,8,64,128]{3,2,1,0:T(8,128)}, u32[]{:S(2)}) copy-start(f32[1,8,64,128]{3,2,1,0:T(8,128)} %param.16) | copy-start | bytes 786436
  6.5 237.3 %all-reduce.6.cloned.1.call-start = ((), (), s32[]{:S(2)}) async-start(), calls=%async_computation | async-start | bytes 524288 | tf_op jit(solution)/shard_map/psum | solution.py:126
  7.8 29.2 %collective-permute-start.2 = (f32[4,64,128]{2,0,1:T(4,128)S(1)}, f32[4,64,128]{2,0,1:T(4,128)S(1)}, u32[]{:S(2)}, u32[]{:S(2)}) collective-permute-start(f32[4,64,128]{2,0,1:T(4,128)S(1)} %get-tuple-element.42), channel_id=1, source_target_pairs={{1,0},{2,1},{3,2},{4,3},{5,4},{6,5},{7,6},{8,7},{9,8},{10,9},{11,1... | collective-permute-start | bytes 393224 | tf_op jit(solution)/shard_map/ppermute | solution.py:18
  9.7 25.3 %copy-start = (f32[8,64,128]{2,1,0:T(8,128)S(1)}, f32[8,64,128]{2,1,0:T(8,128)}, u32[]{:S(2)}) copy-start(f32[8,64,128]{2,1,0:T(8,128)} %param.13) | copy-start | bytes 786436
  9.7 25.3 %copy-start.27 = (f32[1,2,256]{2,1,0:T(2,128)S(1)}, f32[1,2,256]{2,1,0:T(2,128)}, u32[]{:S(2)}) copy-start(f32[1,2,256]{2,1,0:T(2,128)} %param.21) | copy-start | bytes 6148
  9.7 27.2 %copy-start.28 = (s32[1,256]{1,0:T(1,128)S(1)}, s32[1,256]{1,0:T(1,128)}, u32[]{:S(2)}) copy-start(s32[1,256]{1,0:T(1,128)} %param.20) | copy-start | bytes 3076
  9.7 29.2 %collective-permute-start.3 = (f32[4,64,128]{2,0,1:T(4,128)S(1)}, f32[4,64,128]{2,0,1:T(4,128)S(1)}, u32[]{:S(2)}, u32[]{:S(2)}) collective-permute-start(f32[4,64,128]{2,0,1:T(4,128)S(1)} %get-tuple-element.41), channel_id=1, source_target_pairs={{0,1},{1,2},{2,3},{3,4},{4,5},{5,6},{6,7},{7,8},{8,9},{9,10},{10,1... | collective-permute-start | bytes 393224 | tf_op jit(solution)/shard_map/ppermute | solution.py:17
  13.2 32.1 %collective-permute-start.4 = (f32[4,64,128]{2,0,1:T(4,128)}, f32[4,64,128]{2,0,1:T(4,128)S(1)}, u32[]{:S(2)}, u32[]{:S(2)}) collective-permute-start(f32[4,64,128]{2,0,1:T(4,128)} %get-tuple-element.36), channel_id=1, source_target_pairs={{1,0},{2,1},{3,2},{4,3},{5,4},{6,5},{7,6},{8,7},{9,8},{10,9},{11,1... | collective-permute-start | bytes 393224 | tf_op jit(solution)/shard_map/ppermute | solution.py:18
  27.5 17.8 %collective-permute-start.5 = (f32[4,64,128]{2,0,1:T(4,128)}, f32[4,64,128]{2,0,1:T(4,128)S(1)}, u32[]{:S(2)}, u32[]{:S(2)}) collective-permute-start(f32[4,64,128]{2,0,1:T(4,128)} %get-tuple-element.35), channel_id=1, source_target_pairs={{0,1},{1,2},{2,3},{3,4},{4,5},{5,6},{6,7},{7,8},{8,9},{9,10},{10,1... | collective-permute-start | bytes 393224 | tf_op jit(solution)/shard_map/ppermute | solution.py:17
  30.5 11.7 %collective-permute-start = (f32[4,64,128]{2,0,1:T(4,128)}, f32[4,64,128]{2,0,1:T(4,128)S(1)}, u32[]{:S(2)}, u32[]{:S(2)}) collective-permute-start(f32[4,64,128]{2,0,1:T(4,128)} %get-tuple-element.34), channel_id=1, source_target_pairs={{1,0},{2,1},{3,2},{4,3},{5,4},{6,5},{7,6},{8,7},{9,8},{10,9},{11,1... | collective-permute-start | bytes 393224 | tf_op jit(solution)/shard_map/ppermute | solution.py:18
  37.0 7.5 %collective-permute-start.1 = (f32[4,64,128]{2,0,1:T(4,128)}, f32[4,64,128]{2,0,1:T(4,128)S(1)}, u32[]{:S(2)}, u32[]{:S(2)}) collective-permute-start(f32[4,64,128]{2,0,1:T(4,128)} %get-tuple-element.33), channel_id=1, source_target_pairs={{0,1},{1,2},{2,3},{3,4},{4,5},{5,6},{6,7},{7,8},{8,9},{9,10},{10,1... | collective-permute-start | bytes 393224 | tf_op jit(solution)/shard_map/ppermute | solution.py:17
  39.0 6.1 %copy-start.7 = (f32[16,4,128]{2,0,1:T(8,128)}, f32[16,4,128]{2,0,1:T(8,128)S(1)}, u32[]{:S(2)}) copy-start(f32[16,4,128]{2,0,1:T(8,128)S(1)} %reshape.122) | copy-start | bytes 98308
  39.0 6.1 %copy-start.11 = (f32[16,4,128]{2,0,1:T(8,128)}, f32[16,4,128]{2,0,1:T(8,128)S(1)}, u32[]{:S(2)}) copy-start(f32[16,4,128]{2,0,1:T(8,128)S(1)} %reshape.123) | copy-start | bytes 98308
  42.2 3.0 %copy-start.19 = (f32[4,64,128]{2,0,1:T(4,128)}, f32[4,64,128]{2,0,1:T(4,128)S(1)}, u32[]{:S(2)}) copy-start(f32[4,64,128]{2,0,1:T(4,128)S(1)} %collective-permute-done) | copy-start | bytes 393220
  44.5 0.8 copy-start.21
  45.3 1.1 copy-start.23
  45.3 1.1 copy-start.24
  45.3 1.1 copy-start.5
  45.3 1.1 copy-start.8
  45.3 1.1 copy-start.12
  45.3 1.1 copy-start.17
  45.3 1.2 copy-start.26
  46.5 6.1 %copy-start.20 = (f32[4,64,128]{2,0,1:T(4,128)S(1)}, f32[4,64,128]{2,0,1:T(4,128)}, u32[]{:S(2)}) copy-start(f32[4,64,128]{2,0,1:T(4,128)} %copy-done.19) | copy-start | bytes 393220
  46.5 6.1 %copy-start.22 = (f32[4,64,128]{2,0,1:T(4,128)S(1)}, f32[4,64,128]{2,0,1:T(4,128)}, u32[]{:S(2)}) copy-start(f32[4,64,128]{2,0,1:T(4,128)} %copy-done.21) | copy-start | bytes 393220
  46.5 6.1 %copy-start.25 = (f32[1,8,64,128]{3,2,1,0:T(8,128)S(1)}, f32[1,8,64,128]{3,2,1,0:T(8,128)}, u32[]{:S(2)}) copy-start(f32[1,8,64,128]{3,2,1,0:T(8,128)} %param.17) | copy-start | bytes 786436
  56.0 2.1 copy-start.6
  58.0 4.7 %copy-start.18 = (f32[8,64,128]{2,0,1:T(8,128)S(1)}, f32[8,64,128]{2,0,1:T(8,128)}, u32[]{:S(2)}) copy-start(f32[8,64,128]{2,0,1:T(8,128)} %get-tuple-element.17) | copy-start | bytes 786436
  58.4 14.9 %collective-permute-start.8 = (f32[4,64,128]{2,0,1:T(4,128)S(1)}, f32[4,64,128]{2,0,1:T(4,128)S(1)}, u32[]{:S(2)}, u32[]{:S(2)}) collective-permute-start(f32[4,64,128]{2,0,1:T(4,128)S(1)} %get-tuple-element.32), channel_id=1, source_target_pairs={{1,0},{2,1},{3,2},{4,3},{5,4},{6,5},{7,6},{8,7},{9,8},{10,9},{11,1... | collective-permute-start | bytes 393224 | tf_op jit(solution)/shard_map/ppermute | solution.py:18
  60.7 12.6 %collective-permute-start.9 = (f32[4,64,128]{2,0,1:T(4,128)S(1)}, f32[4,64,128]{2,0,1:T(4,128)S(1)}, u32[]{:S(2)}, u32[]{:S(2)}) collective-permute-start(f32[4,64,128]{2,0,1:T(4,128)S(1)} %get-tuple-element.31), channel_id=1, source_target_pairs={{0,1},{1,2},{2,3},{3,4},{4,5},{5,6},{6,7},{7,8},{8,9},{9,10},{10,1... | collective-permute-start | bytes 393224 | tf_op jit(solution)/shard_map/ppermute | solution.py:17
  65.2 14.2 %collective-permute-start.6 = (f32[4,64,128]{2,0,1:T(4,128)}, f32[4,64,128]{2,0,1:T(4,128)}, u32[]{:S(2)}, u32[]{:S(2)}) collective-permute-start(f32[4,64,128]{2,0,1:T(4,128)} %copy.54), channel_id=1, source_target_pairs={{1,0},{2,1},{3,2},{4,3},{5,4},{6,5},{7,6},{8,7},{9,8},{10,9},{11,1... | collective-permute-start | bytes 393224 | tf_op jit(solution)/shard_map/ppermute | solution.py:18
  70.3 10.0 %collective-permute-start.7 = (f32[4,64,128]{2,0,1:T(4,128)}, f32[4,64,128]{2,0,1:T(4,128)}, u32[]{:S(2)}, u32[]{:S(2)}) collective-permute-start(f32[4,64,128]{2,0,1:T(4,128)} %copy.56), channel_id=1, source_target_pairs={{0,1},{1,2},{2,3},{3,4},{4,5},{5,6},{6,7},{7,8},{8,9},{9,10},{10,1... | collective-permute-start | bytes 393224 | tf_op jit(solution)/shard_map/ppermute | solution.py:17
  72.4 1.5 copy-start.2
  72.4 1.5 copy-start.9
  72.4 1.5 copy-start.13
  79.3 2.7 %copy-start.3 = (f32[8,64,128]{2,0,1:T(8,128)S(1)}, f32[8,64,128]{2,0,1:T(8,128)}, u32[]{:S(2)}) copy-start(f32[8,64,128]{2,0,1:T(8,128)} %get-tuple-element.28) | copy-start | bytes 786436
  79.3 2.7 %copy-start.10 = (f32[16,4,128]{2,0,1:T(8,128)S(1)}, f32[16,4,128]{2,0,1:T(8,128)}, u32[]{:S(2)}) copy-start(f32[16,4,128]{2,0,1:T(8,128)} %copy-done.7) | copy-start | bytes 98308
  79.3 2.7 %copy-start.14 = (f32[16,4,128]{2,0,1:T(8,128)S(1)}, f32[16,4,128]{2,0,1:T(8,128)}, u32[]{:S(2)}) copy-start(f32[16,4,128]{2,0,1:T(8,128)} %copy-done.11) | copy-start | bytes 98308
  79.3 2.7 %copy-start.15 = (f32[8,64,128]{2,0,1:T(8,128)S(1)}, f32[8,64,128]{2,0,1:T(8,128)}, u32[]{:S(2)}) copy-start(f32[8,64,128]{2,0,1:T(8,128)} %get-tuple-element.18) | copy-start | bytes 786436
Sparse Core Ops, SparseCore 0:
  87.1 156.7 all-reduce.5
where the time goes:
time: 253 us; the launch traced here: 252 us
  waiting for transfers between devices  159 us (63%)
  starting transfers between devices  37.9 us (15%)
  other arithmetic  27.5 us (11%)
  between operations  16 us (6%)
  local copies, waits for them, and re-layouts  11.8 us (5%)
    psum x1, waiting for transfers between devices, shards(): return lax.psum(gradient, 'shot')  157 us
    ppermute x5, starting transfers between devices, padded_2(): after = lax.ppermute(first, axis, down)  27.4 us
    ppermute x5, starting transfers between devices, padded_2(): before = lax.ppermute(last, axis, up)  10.5 us
    add x2, other arithmetic, shards(): retreated = 2.0 * adjoint - after + operate(padded, buoy_ext)  6.4 us
    add x1, other arithmetic, forward_single(): advanced = 2.0 * field - earlier + stiffness * image  6.13 us
    scatter-add x3, other arithmetic, inject(): flat = field.reshape(-1).at[local_cells].add(amounts, mode='drop')  5.71 us
  transfers between devices with their start and end apart: 11, of which 2 were waited for; matrix products, arithmetic and copies ran while one was open for 7% of the time, Pallas kernels for 0%

commit v1 on v0

v1 whole, which is shorter than its diff:
```python
import jax
import jax.numpy as jnp
from jax import lax
from jax.experimental import pallas as pl
from jax.experimental.pallas import tpu as pltpu
from jax.sharding import PartitionSpec as P

C_SECOND = (-205.0 / 72.0, 8.0 / 5.0, -1.0 / 5.0, 8.0 / 315.0, -1.0 / 560.0)
C_FIRST = (4.0 / 5.0, -1.0 / 5.0, 4.0 / 105.0, -1.0 / 280.0)
MESH = pl.DeviceIdType.MESH
WIDTH = 4
PAD = 8
P_NOW, SQ_NOW, P_NEXT, SQ_NEXT = range(4)


def make_kernel(shots, doms, depth, rows, lanes, receivers):
    plane = rows * lanes
    half = depth // 2
    chunk = half * rows // shots
    per_plane = rows // chunk
    inside = pl.ds(PAD, rows)

    def kernel(
        stiff_hbm,
        buoy_hbm,
        now_hbm,
        prior_hbm,
        adj_hbm,
        after_hbm,
        source_ref,
        wavelet_ref,
        cells_ref,
        traces_ref,
        out_ref,
        buoy,
        fields,
        stiff,
        prior,
        adj,
        after,
        far_halo,
        near_halo,
        slopes,
        base,
        slope_z,
        image,
        adj_next,
        injected,
        grad,
        parts,
        sums,
        load_sem,
        halo_send,
        halo_recv,
        part_send,
        part_recv,
        sum_send,
        sum_recv,
    ):
        shot = lax.axis_index("shot")
        dom = lax.axis_index("dom")
        core = lax.rem(dom, 2)
        near = dom + 1 - 2 * core
        far = dom - 1 + 2 * core
        has_far = (far >= 0) & (far < doms)
        far_count = jnp.where(has_far, 1, 0)
        outer = core * half
        inner = half - outer
        side = (2 * core - 1).astype(jnp.float32)

        barrier = pltpu.get_barrier_semaphore()
        peers = sorted(range(1, shots), key=lambda i: -min(i % 8, 8 - i % 8))

        @pl.when(has_far)
        def _():
            pl.semaphore_signal(barrier, 1, device_id={"dom": far}, device_id_type=MESH)

        pl.semaphore_signal(barrier, 1, device_id={"dom": near}, device_id_type=MESH)
        for i in peers:
            pl.semaphore_signal(
                barrier, 1, device_id={"shot": lax.rem(shot + i, shots)}, device_id_type=MESH
            )

        loads = [
            pltpu.make_async_copy(src, dst, load_sem.at[i])
            for i, (src, dst) in enumerate(
                (
                    (buoy_hbm, buoy.at[pl.ds(WIDTH, depth), inside]),
                    (now_hbm.at[0], fields.at[P_NOW, pl.ds(WIDTH, depth), inside]),
                    (stiff_hbm, stiff),
                    (adj_hbm.at[0], adj),
                    (prior_hbm.at[0], prior),
                    (after_hbm.at[0], after),
                )
            )
        ]
        for load in loads:
            load.start()

        margin = jnp.zeros((PAD, lanes), jnp.float32)
        blank = jnp.zeros((rows, lanes), jnp.float32)

        def clear(f, carry):
            for z in range(WIDTH):
                fields[f, z, inside] = blank
                fields[f, WIDTH + depth + z, inside] = blank
            for z in range(depth):
                fields[f, WIDTH + z, 0:PAD] = margin
                fields[f, WIDTH + z, PAD + rows : 2 * PAD + rows] = margin
            return carry

        lax.fori_loop(0, 4, clear, 0)

        loads[2].wait()
        loads[3].wait()

        def scale(z, carry):
            fields[SQ_NOW, WIDTH + z, inside] = stiff[z] * adj[z]
            return carry

        lax.fori_loop(0, depth, scale, 0)
        loads[0].wait()
        loads[1].wait()

        def far_copy(f):
            if f == 4:
                src = buoy.at[pl.ds(WIDTH + outer, half), inside]
                dst = buoy.at[pl.ds((1 - core) * (WIDTH + depth), half), inside]
            else:
                src = fields.at[f, pl.ds(WIDTH + outer, half), inside]
                dst = far_halo.at[f]
            return pltpu.make_async_remote_copy(
                src, dst, halo_send.at[0, f], halo_recv.at[0, f], device_id={"dom": far}, device_id_type=MESH
            )

        def far_arrival(f):
            if f == 4:
                dst = buoy.at[pl.ds(core * (WIDTH + depth), half), inside]
            else:
                dst = far_halo.at[f]
            return pltpu.make_async_remote_copy(
                dst, dst, halo_send.at[0, f], halo_recv.at[0, f], device_id={"dom": far}, device_id_type=MESH
            )

        def near_copy(f):
            if f == 4:
                src = buoy.at[pl.ds(WIDTH + inner, half), inside]
                dst = buoy.at[pl.ds(core * (WIDTH + depth), half), inside]
            else:
                src = fields.at[f, pl.ds(WIDTH + inner, half), inside]
                dst = near_halo.at[f]
            return pltpu.make_async_remote_copy(
                src, dst, halo_send.at[1, f], halo_recv.at[1, f], device_id={"dom": near}, device_id_type=MESH
            )

        def near_arrival(f):
            if f == 4:
                dst = buoy.at[pl.ds((1 - core) * (WIDTH + depth), half), inside]
            else:
                dst = near_halo.at[f]
            return pltpu.make_async_remote_copy(
                dst, dst, halo_send.at[1, f], halo_recv.at[1, f], device_id={"dom": near}, device_id_type=MESH
            )

        def when_far(act):
            pl.when(has_far)(act)

        pl.semaphore_wait(barrier, shots + far_count)

        for f in (4, P_NOW, SQ_NOW):
            when_far(far_copy(f).start)
        for f in (4, P_NOW, SQ_NOW):
            near_copy(f).start()

        @pl.when(jnp.logical_not(has_far))
        def _():
            edge = buoy[WIDTH + core * (depth - 1), inside]
            for z in range(half):
                buoy[core * (WIDTH + depth) + z, inside] = edge
                for f in range(4):
                    far_halo[f, z] = blank

        lane = lax.broadcasted_iota(jnp.int32, (rows, lanes), 1)

        def buoy_slopes(z, carry):
            here = buoy[WIDTH + z, inside]
            buoy[WIDTH + z, 0:PAD] = jnp.broadcast_to(here[0:1], (PAD, lanes))
            buoy[WIDTH + z, PAD + rows : 2 * PAD + rows] = jnp.broadcast_to(
                here[rows - 1 : rows], (PAD, lanes)
            )
            low = jnp.broadcast_to(here[:, 0:1], (rows, lanes))
            high = jnp.broadcast_to(here[:, lanes - 1 : lanes], (rows, lanes))
            along_x = jnp.zeros_like(here)
            along_y = jnp.zeros_like(here)
            for k in range(1, 5):
                up = buoy[WIDTH + z, PAD + k : PAD + k + rows]
                down = buoy[WIDTH + z, PAD - k : PAD - k + rows]
                along_x = along_x + C_FIRST[k - 1] * (up - down)
                up = jnp.where(lane < lanes - k, pltpu.roll(here, lanes - k, 1), high)
                down = jnp.where(lane >= k, pltpu.roll(here, k, 1), low)
                along_y = along_y + C_FIRST[k - 1] * (up - down)
            slopes[0, z] = along_x
            slopes[1, z] = along_y
            return carry

        lax.fori_loop(0, depth, buoy_slopes, 0)

        def buoy_slope_z(start):
            def body(j, carry):
                z = start + j
                along_z = jnp.zeros((rows, lanes), jnp.float32)
                for k in range(1, 5):
                    up = buoy[WIDTH + z + k, inside]
                    down = buoy[WIDTH + z - k, inside]
                    along_z = along_z + C_FIRST[k - 1] * (up - down)
                slopes[2, z] = along_z
                return carry

            lax.fori_loop(0, half, body, 0)

        def local(f):
            def body(z, carry):
                here = fields[f, WIDTH + z, inside]
                curve = 3.0 * C_SECOND[0] * here
                along = jnp.zeros_like(here)
                for k in range(1, 5):
                    up = fields[f, WIDTH + z + k, inside]
                    down = fields[f, WIDTH + z - k, inside]
                    curve = curve + C_SECOND[k] * (up + down)
                    along = along + C_FIRST[k - 1] * (up - down)
                slope_z[f, z] = along
                along = jnp.zeros_like(here)
                for k in range(1, 5):
                    up = fields[f, WIDTH + z, PAD + k : PAD + k + rows]
                    down = fields[f, WIDTH + z, PAD - k : PAD - k + rows]
                    curve = curve + C_SECOND[k] * (up + down)
                    along = along + C_FIRST[k - 1] * (up - down)
                products = along * slopes[0, z]
                along = jnp.zeros_like(here)
                for k in range(1, 5):
                    up = jnp.where(lane < lanes - k, pltpu.roll(here, lanes - k, 1), 0.0)
                    down = jnp.where(lane >= k, pltpu.roll(here, k, 1), 0.0)
                    curve = curve + C_SECOND[k] * (up + down)
                    along = along + C_FIRST[k - 1] * (up - down)
                products = products + along * slopes[1, z]
                base[f, z] = buoy[WIDTH + z, inside] * curve + products
                return carry

            lax.fori_loop(0, depth, body, 0)

        def whole(f, j, is_far):
            halo = far_halo if is_far else near_halo
            up = core if is_far else 1 - core
            z = up * (depth - 1 - j) + (1 - up) * j
            curve = jnp.zeros((rows, lanes), jnp.float32)
            along = jnp.zeros((rows, lanes), jnp.float32)
            for k in range(j + 1, 5):
                m = k - j
                plane_at = up * (m - 1) + (1 - up) * (half - m)
                value = halo[f, plane_at]
                curve = curve + C_SECOND[k] * value
                along = along + C_FIRST[k - 1] * value
            sign = side if is_far else -side
            along = slope_z[f, z] + sign * along
            return z, base[f, z] + buoy[WIDTH + z, inside] * curve + along * slopes[2, z]

        local_source = source_ref[0] - dom * (depth * plane)
        amplitude = wavelet_ref[0, 0]
        cell = lax.broadcasted_iota(jnp.int32, (rows, lanes), 0) * lanes + lane

        def forward(is_far):
            for j in range(half):
                z, value = whole(P_NOW, j, is_far)
                image[z] = value
                shown = jnp.where(cell + z * plane == local_source, amplitude, 0.0)
                fields[P_NEXT, WIDTH + z, inside] = (
                    2.0 * fields[P_NOW, WIDTH + z, inside] - prior[z] + stiff[z] * value + shown
                )

        def backward(is_far):
            for j in range(half):
                z, value = whole(SQ_NOW, j, is_far)
                value = 2.0 * adj[z] - after[z] + value + injected[z, :, 0:lanes]
                adj_next[z] = value
                fields[SQ_NEXT, WIDTH + z, inside] = stiff[z] * value

        def finish(is_far):
            for j in range(half):
                z, last_image = whole(P_NEXT, j, is_far)
                _, value = whole(SQ_NEXT, j, is_far)
                newer = adj_next[z]
                value = 2.0 * newer - adj[z] + value + injected[z, :, lanes : 2 * lanes]
                grad[z] = newer * last_image + value * image[z]

        local_cells = cells_ref[...] - dom * (depth * plane)
        cell_rows = jnp.right_shift(local_cells, 7)
        cell_lanes = jnp.bitwise_and(local_cells, lanes - 1)
        lane_hot = lax.broadcasted_iota(jnp.int32, (lanes, receivers), 0) == cell_lanes
        amounts = jnp.concatenate(
            [jnp.where(lane_hot, traces_ref[0, k : k + 1, :], 0.0) for k in range(2)], axis=0
        )
        high = amounts.astype(jnp.bfloat16)
        rest = amounts - high.astype(jnp.float32)
        middle = rest.astype(jnp.bfloat16)
        low = (rest - middle.astype(jnp.float32)).astype(jnp.bfloat16)

        def inject(z, carry):
            row = lax.broadcasted_iota(jnp.int32, (rows, receivers), 0) + z * rows
            row_hot = jnp.where(row == cell_rows, 1.0, 0.0).astype(jnp.bfloat16)
            total = jnp.zeros((rows, 2 * lanes), jnp.float32)
            for part in (low, middle, high):
                total = total + lax.dot_general(
                    row_hot, part, (((1,), (1,)), ((), ())), preferred_element_type=jnp.float32
                )
            injected[z] = total
            return carry

        def reduce_start(h, start):
            for i in peers:
                peer = lax.rem(shot + i, shots)
                src = grad.at[start + peer // per_plane, pl.ds(lax.rem(peer, per_plane) * chunk, chunk)]
                pltpu.make_async_remote_copy(
                    src, parts.at[h, shot], part_send.at[h, i], part_recv.at[h, i],
                    device_id={"shot": peer}, device_id_type=MESH,
                ).start()

        def reduce_finish(h, start):
            total = grad[start + shot // per_plane, pl.ds(lax.rem(shot, per_plane) * chunk, chunk)]
            for i in peers:
                peer = lax.rem(shot + shots - i, shots)
                pltpu.make_async_remote_copy(
                    parts.at[h, peer], parts.at[h, peer], part_send.at[h, i], part_recv.at[h, i],
                    device_id={"shot": peer}, device_id_type=MESH,
                ).wait_recv()
                total = total + parts[h, peer]
            sums[h] = total
            dst = out_ref.at[start + shot // per_plane, pl.ds(lax.rem(shot, per_plane) * chunk, chunk)]
            for i in peers:
                peer = lax.rem(shot + i, shots)
                pltpu.make_async_remote_copy(
                    sums.at[h], dst, sum_send.at[h, i], sum_recv.at[h, i],
                    device_id={"shot": peer}, device_id_type=MESH,
                ).start()
            pltpu.make_async_copy(sums.at[h], dst, load_sem.at[h]).start()

        def reduce_drain(h, start):
            pltpu.make_async_copy(sums.at[h], out_ref.at[0, pl.ds(0, chunk)], load_sem.at[h]).wait()
            for i in peers:
                peer = lax.rem(shot + shots - i, shots)
                dst = out_ref.at[start + peer // per_plane, pl.ds(lax.rem(peer, per_plane) * chunk, chunk)]
                copy = pltpu.make_async_remote_copy(
                    sums.at[h], dst, sum_send.at[h, i], sum_recv.at[h, i],
                    device_id={"shot": peer}, device_id_type=MESH,
                )
                copy.wait_recv()
                copy.wait_send()
                pltpu.make_async_remote_copy(
                    parts.at[h, peer], parts.at[h, peer], part_send.at[h, i], part_recv.at[h, i],
                    device_id={"shot": peer}, device_id_type=MESH,
                ).wait_send()

        local(P_NOW)
        local(SQ_NOW)
        lax.fori_loop(0, depth, inject, 0)
        loads[4].wait()
        loads[5].wait()

        near_arrival(4).wait_recv()
        buoy_slope_z(inner)
        near_arrival(P_NOW).wait_recv()
        forward(False)
        near_copy(P_NEXT).start()
        near_arrival(SQ_NOW).wait_recv()
        backward(False)
        near_copy(SQ_NEXT).start()

        when_far(far_arrival(4).wait_recv)
        buoy_slope_z(outer)
        when_far(far_arrival(P_NOW).wait_recv)
        forward(True)
        when_far(far_copy(P_NEXT).start)
        when_far(far_arrival(SQ_NOW).wait_recv)
        backward(True)
        when_far(far_copy(SQ_NEXT).start)

        local(P_NEXT)
        local(SQ_NEXT)
        near_arrival(P_NEXT).wait_recv()
        near_arrival(SQ_NEXT).wait_recv()
        finish(False)
        reduce_start(0, inner)
        when_far(far_arrival(P_NEXT).wait_recv)
        when_far(far_arrival(SQ_NEXT).wait_recv)
        finish(True)
        reduce_start(1, outer)
        reduce_finish(0, inner)
        reduce_finish(1, outer)
        for f in range(5):
            when_far(far_copy(f).wait_send)
            near_copy(f).wait_send()
        reduce_drain(0, inner)
        reduce_drain(1, outer)

    return kernel


def solution(mesh):
    shots, doms = mesh.shape["shot"], mesh.shape["dom"]

    def shards(
        stiffness,
        buoyancy,
        forward_now,
        forward_prior,
        adjoint_now,
        adjoint_after,
        source_cells,
        wavelet,
        receiver_cells,
        residuals,
    ):
        depth, rows, lanes = stiffness.shape
        receivers = receiver_cells.shape[1]
        half = depth // 2
        chunk = half * rows // shots
        padded = (depth + 2 * WIDTH, rows + 2 * PAD, lanes)
        slab = (depth, rows, lanes)
        f32 = jnp.float32
        in_hbm = pl.BlockSpec(memory_space=pltpu.HBM)
        in_smem = pl.BlockSpec(memory_space=pltpu.SMEM)
        in_vmem = pl.BlockSpec(memory_space=pltpu.VMEM)
        return pl.pallas_call(
            make_kernel(shots, doms, depth, rows, lanes, receivers),
            out_shape=jax.ShapeDtypeStruct(slab, f32),
            in_specs=[in_hbm] * 6 + [in_smem] * 2 + [in_vmem] * 2,
            out_specs=in_hbm,
            scratch_shapes=[
                pltpu.VMEM(padded, f32),
                pltpu.VMEM((4, *padded), f32),
                pltpu.VMEM(slab, f32),
                pltpu.VMEM(slab, f32),
                pltpu.VMEM(slab, f32),
                pltpu.VMEM(slab, f32),
                pltpu.VMEM((4, half, rows, lanes), f32),
                pltpu.VMEM((4, half, rows, lanes), f32),
                pltpu.VMEM((3, *slab), f32),
                pltpu.VMEM((4, *slab), f32),
                pltpu.VMEM((4, *slab), f32),
                pltpu.VMEM(slab, f32),
                pltpu.VMEM(slab, f32),
                pltpu.VMEM((depth, rows, 2 * lanes), f32),
                pltpu.VMEM(slab, f32),
                pltpu.VMEM((2, shots, chunk, lanes), f32),
                pltpu.VMEM((2, chunk, lanes), f32),
                pltpu.SemaphoreType.DMA((6,)),
                pltpu.SemaphoreType.DMA((2, 5)),
                pltpu.SemaphoreType.DMA((2, 5)),
                pltpu.SemaphoreType.DMA((2, shots)),
                pltpu.SemaphoreType.DMA((2, shots)),
                pltpu.SemaphoreType.DMA((2, shots)),
                pltpu.SemaphoreType.DMA((2, shots)),
            ],
            compiler_params=pltpu.CompilerParams(
                collective_id=0, has_side_effects=True, vmem_limit_bytes=48 * 1024 * 1024
            ),
            name="window",
        )(
            stiffness, buoyancy, forward_now, forward_prior, adjoint_now, adjoint_after,
            source_cells, wavelet, receiver_cells, residuals,
        )

    placed = (
        P("dom", None, None),
        P("dom", None, None),
        P("shot", "dom", None, None),
        P("shot", "dom", None, None),
        P("shot", "dom", None, None),
        P("shot", "dom", None, None),
        P("shot"),
        P("shot", None),
        P("shot", None),
        P("shot", None, None),
    )
    return jax.shard_map(
        shards, mesh=mesh, in_specs=placed, out_specs=P("dom", None, None), check_vma=False
    )
```

time: 253 us -> 49.8 us (0.20)
  the two profiles are of different devices: /device:TPU:32 before, /device:TPU:497 now
where the time goes in v1:
time: 49.8 us; the launch traced here: 49.4 us
  Pallas kernels  41.7 us (84%)
  local copies, waits for them, and re-layouts  6.4 us (13%)
  between operations  1.37 us (3%)
    pallas_call x1, Pallas kernels, shards(): pl.pallas_call(make_kernel(shots, doms, depth, rows, lanes, receivers), o...  41.7 us
    unnamed x17, local copies, waits for them, and re-layouts  6.4 us

profile of v1, /device:TPU:497, one launch (start us, length us, event | category | flops | bytes accessed | tf_op | source)
XLA Modules:
  0.0 49.4 jit_solution(8022048124930577109)
XLA Ops:
  0.0 0.0 copy-start.6
  0.7 0.0 copy-start.7
  1.3 0.0 copy-done.6
  1.3 0.0 copy-done.7
  1.4 0.0 copy-start
  1.4 0.9 %copy-done = f32[8,64,128]{2,1,0:T(8,128)S(1)} copy-done((f32[8,64,128]{2,1,0:T(8,128)S(1)}, f32[8,64,128]{2,1,0:T(8,128)}, u32[]{:S(2)}) %copy-start) | copy-done | bytes 262168
  2.3 0.0 copy-start.1
  2.3 0.9 %copy-done.1 = f32[8,64,128]{2,1,0:T(8,128)S(1)} copy-done((f32[8,64,128]{2,1,0:T(8,128)S(1)}, f32[8,64,128]{2,1,0:T(8,128)}, u32[]{:S(2)}) %copy-start.1) | copy-done | bytes 262168
  3.3 0.0 copy-start.2
  3.3 0.9 %copy-done.2 = f32[1,8,64,128]{3,2,1,0:T(8,128)S(1)} copy-done((f32[1,8,64,128]{3,2,1,0:T(8,128)S(1)}, f32[1,8,64,128]{3,2,1,0:T(8,128)}, u32[]{:S(2)}) %copy-start.2) | copy-done | bytes 262168
  4.2 0.0 copy-start.3
  4.2 0.9 %copy-done.3 = f32[1,8,64,128]{3,2,1,0:T(8,128)S(1)} copy-done((f32[1,8,64,128]{3,2,1,0:T(8,128)S(1)}, f32[1,8,64,128]{3,2,1,0:T(8,128)}, u32[]{:S(2)}) %copy-start.3) | copy-done | bytes 262168
  5.2 0.0 copy-start.4
  5.2 0.9 %copy-done.4 = f32[1,8,64,128]{3,2,1,0:T(8,128)S(1)} copy-done((f32[1,8,64,128]{3,2,1,0:T(8,128)S(1)}, f32[1,8,64,128]{3,2,1,0:T(8,128)}, u32[]{:S(2)}) %copy-start.4) | copy-done | bytes 262168
  6.1 0.0 copy-start.5
  6.1 0.9 %copy-done.5 = f32[1,8,64,128]{3,2,1,0:T(8,128)S(1)} copy-done((f32[1,8,64,128]{3,2,1,0:T(8,128)S(1)}, f32[1,8,64,128]{3,2,1,0:T(8,128)}, u32[]{:S(2)}) %copy-start.5) | copy-done | bytes 262168
  7.1 41.7 %window.1 = f32[8,64,128]{2,1,0:T(8,128)S(1)} custom-call(f32[8,64,128]{2,1,0:T(8,128)S(1)} %copy-done, f32[8,64,128]{2,1,0:T(8,128)S(1)} %copy-done.1, f32[1,8,64,128]{3,2,1,0:T(8,128)S(1)} %copy-done.2, f32[1,8,64,128]{3,2,1,0:T(8,128)S(1)} %copy-done.3, f32[1,8,64,128]{3,2,1,0:T(8,128)S(1)} %copy-done.4, f32[1,8,64,128]{3,2,1,0:T(8,128)S(1)} %copy-done.5, ...), custom_call_target="tpu_custom_call" | custom-call | tf_op jit(solution)/shard_map/window/pallas_call | solution.py:432
  48.7 0.7 %copy.14 = f32[8,64,128]{2,1,0:T(8,128)} copy(f32[8,64,128]{2,1,0:T(8,128)S(1)} %window.1) | data formatting | bytes 524288
Async XLA Ops:
  0.0 1.3 %copy-start.6 = (f32[1,2,256]{2,1,0:T(2,128)S(1)}, f32[1,2,256]{2,1,0:T(2,128)}, u32[]{:S(2)}) copy-start(f32[1,2,256]{2,1,0:T(2,128)} %traces_ref.1) | copy-start | bytes 6148
  0.7 0.7 %copy-start.7 = (s32[1,256]{1,0:T(1,128)S(1)}, s32[1,256]{1,0:T(1,128)}, u32[]{:S(2)}) copy-start(s32[1,256]{1,0:T(1,128)} %cells_ref.1) | copy-start | bytes 3076
  1.4 1.0 %copy-start = (f32[8,64,128]{2,1,0:T(8,128)S(1)}, f32[8,64,128]{2,1,0:T(8,128)}, u32[]{:S(2)}) copy-start(f32[8,64,128]{2,1,0:T(8,128)} %stiff_hbm.1) | copy-start | bytes 786436
  2.3 0.9 %copy-start.1 = (f32[8,64,128]{2,1,0:T(8,128)S(1)}, f32[8,64,128]{2,1,0:T(8,128)}, u32[]{:S(2)}) copy-start(f32[8,64,128]{2,1,0:T(8,128)} %buoy_hbm.1) | copy-start | bytes 786436
  3.3 0.9 %copy-start.2 = (f32[1,8,64,128]{3,2,1,0:T(8,128)S(1)}, f32[1,8,64,128]{3,2,1,0:T(8,128)}, u32[]{:S(2)}) copy-start(f32[1,8,64,128]{3,2,1,0:T(8,128)} %now_hbm.1) | copy-start | bytes 786436
  4.2 0.9 %copy-start.3 = (f32[1,8,64,128]{3,2,1,0:T(8,128)S(1)}, f32[1,8,64,128]{3,2,1,0:T(8,128)}, u32[]{:S(2)}) copy-start(f32[1,8,64,128]{3,2,1,0:T(8,128)} %prior_hbm.1) | copy-start | bytes 786436
  5.2 0.9 %copy-start.4 = (f32[1,8,64,128]{3,2,1,0:T(8,128)S(1)}, f32[1,8,64,128]{3,2,1,0:T(8,128)}, u32[]{:S(2)}) copy-start(f32[1,8,64,128]{3,2,1,0:T(8,128)} %adj_hbm.1) | copy-start | bytes 786436
  6.1 0.9 %copy-start.5 = (f32[1,8,64,128]{3,2,1,0:T(8,128)S(1)}, f32[1,8,64,128]{3,2,1,0:T(8,128)}, u32[]{:S(2)}) copy-start(f32[1,8,64,128]{3,2,1,0:T(8,128)} %after_hbm.1) | copy-start | bytes 786436

commit v2 on v1

v2 whole, which is shorter than its diff:
```python
import jax
import jax.numpy as jnp
from jax import lax
from jax.experimental import pallas as pl
from jax.experimental.pallas import tpu as pltpu
from jax.sharding import PartitionSpec as P

C_SECOND = (-205.0 / 72.0, 8.0 / 5.0, -1.0 / 5.0, 8.0 / 315.0, -1.0 / 560.0)
C_FIRST = (4.0 / 5.0, -1.0 / 5.0, 4.0 / 105.0, -1.0 / 280.0)
MESH = pl.DeviceIdType.MESH
WIDTH = 4
P_NOW, SQ_NOW, P_NEXT, SQ_NEXT = range(4)


def make_kernel(shots, doms, depth, rows, lanes, receivers):
    plane = rows * lanes
    half = depth // 2
    length = shots // 2
    chunk = half * rows // shots
    wide = half * rows // length
    steps = sorted({1, length - 1})
    leaps = sorted({2 % length, (length - 2) % length} - {0})

    def kernel(
        stiff_hbm,
        buoy_hbm,
        now_hbm,
        prior_hbm,
        adj_hbm,
        after_hbm,
        source_ref,
        wavelet_ref,
        cells_ref,
        traces_ref,
        out_ref,
        buoy,
        fields,
        stiff,
        prior,
        adj,
        after,
        far_halo,
        near_halo,
        slopes,
        base,
        slope_z,
        image,
        adj_next,
        injected,
        left,
        right,
        grad,
        parts,
        sums,
        wide_parts,
        wide_sums,
        load_sem,
        halo_send,
        halo_recv,
        outer_send,
        outer_recv,
        inner_send,
        inner_recv,
        near_ready,
        greeted,
    ):
        shot = lax.axis_index("shot")
        dom = lax.axis_index("dom")
        core = lax.rem(dom, 2)
        near = dom + 1 - 2 * core
        far = dom - 1 + 2 * core
        has_far = (far >= 0) & (far < doms)
        far_count = jnp.where(has_far, 1, 0)
        outer = core * half
        inner = half - outer
        side = (2 * core - 1).astype(jnp.float32)

        row, column = shot // length, lax.rem(shot, length)

        def along(i):
            return {"shot": row * length + lax.rem(column + i, length)}

        across = {"shot": (1 - row) * length + column}
        peers = sorted(range(1, shots), key=lambda i: -min(i % length, length - i % length))
        line = sorted(range(1, length), key=lambda i: -min(i, length - i))

        barrier = pltpu.get_barrier_semaphore()

        @pl.when(has_far)
        def _():
            pl.semaphore_signal(barrier, 1, device_id={"dom": far}, device_id_type=MESH)

        @pl.when(core == 1)
        def _():
            pl.semaphore_signal(barrier, 1, device_id={"dom": near}, device_id_type=MESH)

        for i in steps:
            pl.semaphore_signal(barrier, 1, device_id=along(i), device_id_type=MESH)
        pl.semaphore_signal(barrier, 1, device_id=across, device_id_type=MESH)

        loads = [
            pltpu.make_async_copy(src, dst, load_sem.at[i])
            for i, (src, dst) in enumerate(
                (
                    (buoy_hbm, buoy.at[pl.ds(WIDTH, depth)]),
                    (now_hbm.at[0], fields.at[P_NOW, pl.ds(WIDTH, depth)]),
                    (stiff_hbm, stiff),
                    (adj_hbm.at[0], adj),
                    (prior_hbm.at[0], prior),
                    (after_hbm.at[0], after),
                )
            )
        ]
        for load in loads:
            load.start()

        blank = jnp.zeros((rows, lanes), jnp.float32)

        def clear(f, carry):
            for z in range(WIDTH):
                fields[f, z] = blank
                fields[f, WIDTH + depth + z] = blank
            return carry

        lax.fori_loop(0, 4, clear, 0)

        def split(value):
            high = value.astype(jnp.bfloat16)
            return high, (value - high.astype(jnp.float32)).astype(jnp.bfloat16)

        def second(offset):
            total = jnp.zeros(offset.shape, jnp.float32)
            for k in range(1, 5):
                total = jnp.where(jnp.abs(offset) == k, C_SECOND[k], total)
            return total

        def first(offset):
            total = jnp.zeros(offset.shape, jnp.float32)
            for k in range(1, 5):
                total = jnp.where(offset == k, C_FIRST[k - 1], total)
                total = jnp.where(offset == -k, -C_FIRST[k - 1], total)
            return total

        def first_extended(source, target, length):
            total = jnp.zeros(source.shape, jnp.float32)
            for k in range(1, 5):
                up = jnp.minimum(target + k, length - 1)
                down = jnp.maximum(target - k, 0)
                total = total + jnp.where(source == up, C_FIRST[k - 1], 0.0)
                total = total - jnp.where(source == down, C_FIRST[k - 1], 0.0)
            return total

        def make_matrices():
            source = lax.broadcasted_iota(jnp.int32, (lanes, lanes), 0)
            target = lax.broadcasted_iota(jnp.int32, (lanes, lanes), 1)
            offset = source - target
            centre = jnp.where(offset == 0, 3.0 * C_SECOND[0], 0.0)
            for at, value in enumerate(
                (second(offset) + centre, first(offset), first_extended(source, target, lanes))
            ):
                columns = pl.ds(at * lanes, lanes)
                high, low = split(value)
                right[0:lanes, columns] = high
                right[lanes : 2 * lanes, columns] = high
                right[2 * lanes : 3 * lanes, columns] = low
            target = lax.broadcasted_iota(jnp.int32, (rows, 3 * rows), 0)
            source = lax.rem(lax.broadcasted_iota(jnp.int32, (rows, 3 * rows), 1), rows)
            last = lax.broadcasted_iota(jnp.int32, (rows, 3 * rows), 1) >= 2 * rows
            offset = source - target
            for at, value in enumerate(
                (second(offset), first(offset), first_extended(source, target, rows))
            ):
                high, low = split(value)
                left[at * rows : (at + 1) * rows] = jnp.where(
                    last, low.astype(jnp.float32), high.astype(jnp.float32)
                ).astype(jnp.bfloat16)

        make_matrices()

        def dot(a, b):
            return lax.dot_general(
                a, b, (((1,), (0,)), ((), ())), preferred_element_type=jnp.float32
            )

        def differences(value, which):
            high, low = split(value)
            flat_high = high.reshape(2 * rows, lanes)
            flat = jnp.concatenate([flat_high, low.reshape(2 * rows, lanes)], axis=1)
            first_column, columns = (0, 2 * lanes) if which == 0 else (2 * lanes, lanes)
            use = pl.ds(first_column, columns)
            along_y = dot(flat, right[0 : 2 * lanes, use]) + dot(
                flat_high, right[2 * lanes : 3 * lanes, use]
            )
            stacked = jnp.concatenate(
                [jnp.concatenate([high[i], low[i], high[i]], axis=0) for i in range(2)], axis=1
            )
            use = pl.ds(0, 2 * rows) if which == 0 else pl.ds(2 * rows, rows)
            along_x = dot(left[use], stacked)
            return along_x, along_y

        loads[2].wait()
        loads[3].wait()

        def scale(z, carry):
            fields[SQ_NOW, WIDTH + z] = stiff[z] * adj[z]
            return carry

        lax.fori_loop(0, depth, scale, 0)
        loads[0].wait()
        loads[1].wait()

        def far_copy(f):
            if f == 4:
                src = buoy.at[pl.ds(WIDTH + outer, half)]
                dst = buoy.at[pl.ds((1 - core) * (WIDTH + depth), half)]
            else:
                src = fields.at[f, pl.ds(WIDTH + outer, half)]
                dst = far_halo.at[f]
            return pltpu.make_async_remote_copy(
                src, dst, halo_send.at[0, f], halo_recv.at[0, f], device_id={"dom": far}, device_id_type=MESH
            )

        def far_arrival(f):
            if f == 4:
                dst = buoy.at[pl.ds(core * (WIDTH + depth), half)]
            else:
                dst = far_halo.at[f]
            return pltpu.make_async_remote_copy(
                dst, dst, halo_send.at[0, f], halo_recv.at[0, f], device_id={"dom": far}, device_id_type=MESH
            )

        def near_copy(f):
            if f == 4:
                src = buoy.at[pl.ds(WIDTH + inner, half)]
                dst = buoy.at[pl.ds(core * (WIDTH + depth), half)]
            else:
                src = fields.at[f, pl.ds(WIDTH + inner, half)]
                dst = near_halo.at[f]
            return pltpu.make_async_remote_copy(
                src, dst, halo_send.at[1, f], halo_recv.at[1, f], device_id={"dom": near}, device_id_type=MESH
            )

        def near_arrival(f):
            if f == 4:
                dst = buoy.at[pl.ds((1 - core) * (WIDTH + depth), half)]
            else:
                dst = near_halo.at[f]
            return pltpu.make_async_remote_copy(
                dst, dst, halo_send.at[1, f], halo_recv.at[1, f], device_id={"dom": near}, device_id_type=MESH
            )

        def when_far(act):
            pl.when(has_far)(act)

        def buoy_slopes():
            for z in range(0, depth, 2):
                along_x, along_y = differences(buoy[WIDTH + z : WIDTH + z + 2], 1)
                for i in range(2):
                    slopes[0, z + i] = along_x[:, i * lanes : (i + 1) * lanes]
                    slopes[1, z + i] = along_y[i * rows : (i + 1) * rows]

        def buoy_slope_z(start):
            def body(j, carry):
                z = start + j
                along_z = jnp.zeros((rows, lanes), jnp.float32)
                for k in range(1, 5):
                    up = buoy[WIDTH + z + k]
                    down = buoy[WIDTH + z - k]
                    along_z = along_z + C_FIRST[k - 1] * (up - down)
                slopes[2, z] = along_z
                return carry

            lax.fori_loop(0, half, body, 0)

        def local(f):
            for z0 in range(0, depth, 2):
                along_x, along_y = differences(fields[f, WIDTH + z0 : WIDTH + z0 + 2], 0)
                for i in range(2):
                    z = z0 + i
                    of_x = slice(i * lanes, (i + 1) * lanes)
                    of_y = slice(i * rows, (i + 1) * rows)
                    curve = along_x[0:rows, of_x] + along_y[of_y, 0:lanes]
                    along = jnp.zeros((rows, lanes), jnp.float32)
                    for k in range(1, 5):
                        up = fields[f, WIDTH + z + k]
                        down = fields[f, WIDTH + z - k]
                        curve = curve + C_SECOND[k] * (up + down)
                        along = along + C_FIRST[k - 1] * (up - down)
                    slope_z[f, z] = along
                    base[f, z] = (
                        buoy[WIDTH + z] * curve
                        + along_x[rows : 2 * rows, of_x] * slopes[0, z]
                        + along_y[of_y, lanes : 2 * lanes] * slopes[1, z]
                    )

        buoy_slopes()
        local(P_NOW)
        local(SQ_NOW)
        pl.semaphore_wait(barrier, len(steps) + 1 + far_count + (1 - core))

        for f in (4, P_NOW, SQ_NOW):
            when_far(far_copy(f).start)

        def near_begin():
            @pl.when(core == 0)
            def _():
                pl.semaphore_signal(near_ready, 1, device_id={"dom": near}, device_id_type=MESH)

            @pl.when(core == 1)
            def _():
                pl.semaphore_wait(near_ready, 1)

            for f in (4, P_NOW, SQ_NOW):
                near_copy(f).start()

        pl.when(dom != 1)(near_begin)
        for i in steps:
            pl.semaphore_signal(greeted.at[0], 1, device_id=along(i), device_id_type=MESH)

        @pl.when(jnp.logical_not(has_far))
        def _():
            edge = buoy[WIDTH + core * (depth - 1)]
            for z in range(half):
                buoy[core * (WIDTH + depth) + z] = edge
                for f in range(4):
                    far_halo[f, z] = blank

        def whole(f, j, is_far):
            halo = far_halo if is_far else near_halo
            up = core if is_far else 1 - core
            z = up * (depth - 1 - j) + (1 - up) * j
            curve = jnp.zeros((rows, lanes), jnp.float32)
            along = jnp.zeros((rows, lanes), jnp.float32)
            for k in range(j + 1, 5):
                m = k - j
                plane_at = up * (m - 1) + (1 - up) * (half - m)
                value = halo[f, plane_at]
                curve = curve + C_SECOND[k] * value
                along = along + C_FIRST[k - 1] * value
            sign = side if is_far else -side
            along = slope_z[f, z] + sign * along
            return z, base[f, z] + buoy[WIDTH + z] * curve + along * slopes[2, z]

        for load in loads[4:]:
            load.wait()
        local_source = source_ref[...].reshape(1, 1) - dom * (depth * plane)
        amplitude = wavelet_ref[...]
        cell = lax.broadcasted_iota(jnp.int32, (rows, lanes), 0) * lanes
        cell = cell + lax.broadcasted_iota(jnp.int32, (rows, lanes), 1)

        def forward(is_far):
            for j in range(half):
                z, value = whole(P_NOW, j, is_far)
                image[z] = value
                shown = jnp.where(cell + z * plane == local_source, amplitude, 0.0)
                fields[P_NEXT, WIDTH + z] = (
                    2.0 * fields[P_NOW, WIDTH + z] - prior[z] + stiff[z] * value + shown
                )

        def backward(is_far):
            for j in range(half):
                z, value = whole(SQ_NOW, j, is_far)
                value = 2.0 * adj[z] - after[z] + value + injected[pl.ds(z * rows, rows), 0:lanes]
                adj_next[z] = value
                fields[SQ_NEXT, WIDTH + z] = stiff[z] * value

        def finish(is_far):
            for j in range(half):
                z, last_image = whole(P_NEXT, j, is_far)
                _, value = whole(SQ_NEXT, j, is_far)
                newer = adj_next[z]
                value = 2.0 * newer - adj[z] + value + injected[pl.ds(z * rows, rows), lanes : 2 * lanes]
                grad[pl.ds(z * rows, rows)] = newer * last_image + value * image[z]

        def inject():
            local_cells = cells_ref[...] - dom * (depth * plane)
            cell_rows = jnp.right_shift(local_cells, 7)
            cell_lanes = jnp.bitwise_and(local_cells, lanes - 1)
            lane_hot = lax.broadcasted_iota(jnp.int32, (lanes, receivers), 0) == cell_lanes
            amounts = jnp.concatenate(
                [jnp.where(lane_hot, traces_ref[0, k : k + 1, :], 0.0) for k in range(2)], axis=0
            )
            amounts = amounts.T
            high, _ = split(amounts)
            middle, low = split(amounts - high.astype(jnp.float32))
            row = lax.broadcasted_iota(jnp.int32, (depth * rows, receivers), 0)
            row_hot = jnp.where(row == cell_rows, 1.0, 0.0).astype(jnp.bfloat16)
            injected[...] = dot(row_hot, low) + dot(row_hot, middle) + dot(row_hot, high)

        def share(of):
            return pl.ds(outer * rows + of * chunk, chunk)

        def outer_copy(stage, i):
            peer = lax.rem(shot + i, shots)
            if stage == 0:
                src, dst = grad.at[share(peer)], parts.at[shot]
            else:
                src, dst = sums, out_ref.at[share(shot)]
            return pltpu.make_async_remote_copy(
                src, dst, outer_send.at[stage], outer_recv.at[stage], device_id={"shot": peer}, device_id_type=MESH
            )

        def outer_all(stage):
            every = parts.at[pl.ds(0, shots - 1)]
            return pltpu.make_async_remote_copy(
                every, every, outer_send.at[stage], outer_recv.at[stage], device_id=across, device_id_type=MESH
            )

        def wide_share(of):
            return pl.ds(inner * rows + of * wide, wide)

        def inner_copy(stage, i):
            peer = lax.rem(column + i, length)
            if stage == 0:
                src, dst = grad.at[wide_share(peer)], wide_parts.at[column]
            else:
                src, dst = wide_sums.at[2], out_ref.at[wide_share(column)]
            return pltpu.make_async_remote_copy(
                src, dst, inner_send.at[stage], inner_recv.at[stage], device_id=along(i), device_id_type=MESH
            )

        def inner_all(stage):
            every = wide_parts.at[pl.ds(0, length - 1)]
            return pltpu.make_async_remote_copy(
                every, every, inner_send.at[stage], inner_recv.at[stage], device_id=across, device_id_type=MESH
            )

        swap = pltpu.make_async_remote_copy(
            wide_sums.at[0], wide_sums.at[1], inner_send.at[2], inner_recv.at[2], device_id=across, device_id_type=MESH
        )

        def near_fold():
            near_arrival(4).wait_recv()
            buoy_slope_z(inner)
            near_arrival(P_NOW).wait_recv()
            forward(False)
            near_copy(P_NEXT).start()
            near_arrival(SQ_NOW).wait_recv()
            backward(False)
            near_copy(SQ_NEXT).start()

        inject()

        when_far(far_arrival(4).wait_recv)
        buoy_slope_z(outer)
        when_far(far_arrival(P_NOW).wait_recv)
        forward(True)
        when_far(far_copy(P_NEXT).start)

        pl.semaphore_wait(greeted.at[0], len(steps))
        for i in leaps:
            pl.semaphore_signal(greeted.at[1], 1, device_id=along(i), device_id_type=MESH)
        pl.when(dom != 1)(near_fold)

        when_far(far_arrival(SQ_NOW).wait_recv)
        backward(True)
        when_far(far_copy(SQ_NEXT).start)

        @pl.when(dom == 1)
        def _():
            near_begin()
            near_fold()

        if leaps:
            pl.semaphore_wait(greeted.at[1], len(leaps))
        pl.semaphore_signal(greeted.at[2], 1, device_id=across, device_id_type=MESH)

        local(P_NEXT)
        local(SQ_NEXT)
        near_arrival(P_NEXT).wait_recv()
        near_arrival(SQ_NEXT).wait_recv()
        finish(False)
        for i in line:
            inner_copy(0, i).start()
        pl.semaphore_wait(greeted.at[2], 1)

        when_far(far_arrival(P_NEXT).wait_recv)
        when_far(far_arrival(SQ_NEXT).wait_recv)
        finish(True)
        for i in peers:
            outer_copy(0, i).start()

        inner_all(0).wait_recv()
        total = grad[wide_share(column)]
        for i in line:
            total = total + wide_parts[lax.rem(column + i, length)]
        wide_sums[0] = total
        swap.start()
        swap.wait_recv()
        wide_sums[2] = wide_sums[0] + wide_sums[1]
        for i in line:
            inner_copy(1, i).start()
        out_ref[wide_share(column)] = wide_sums[2]

        outer_all(0).wait_recv()
        total = grad[share(shot)]
        for i in peers:
            total = total + parts[lax.rem(shot + i, shots)]
        sums[...] = total
        for i in peers:
            outer_copy(1, i).start()
        out_ref[share(shot)] = total

        for f in range(5):
            when_far(far_copy(f).wait_send)
            near_copy(f).wait_send()
        swap.wait_send()
        for stage in range(2):
            inner_all(stage).wait_send()
        outer_all(0).wait_send()
        inner_all(1).wait_recv()
        outer_all(1).wait_send()
        outer_all(1).wait_recv()

    return kernel


def solution(mesh):
    shots, doms = mesh.shape["shot"], mesh.shape["dom"]

    def shards(
        stiffness,
        buoyancy,
        forward_now,
        forward_prior,
        adjoint_now,
        adjoint_after,
        source_cells,
        wavelet,
        receiver_cells,
        residuals,
    ):
        depth, rows, lanes = stiffness.shape
        receivers = receiver_cells.shape[1]
        half = depth // 2
        length = shots // 2
        chunk = half * rows // shots
        wide = half * rows // length
        padded = (depth + 2 * WIDTH, rows, lanes)
        slab = (depth, rows, lanes)
        f32 = jnp.float32
        in_hbm = pl.BlockSpec(memory_space=pltpu.HBM)
        return pl.pallas_call(
            make_kernel(shots, doms, depth, rows, lanes, receivers),
            out_shape=jax.ShapeDtypeStruct((depth * rows, lanes), f32),
            in_specs=[in_hbm] * 6 + [pl.BlockSpec(memory_space=pltpu.VMEM)] * 4,
            out_specs=pl.BlockSpec(memory_space=pltpu.VMEM),
            scratch_shapes=[
                pltpu.VMEM(padded, f32),
                pltpu.VMEM((4, *padded), f32),
                pltpu.VMEM(slab, f32),
                pltpu.VMEM(slab, f32),
                pltpu.VMEM(slab, f32),
                pltpu.VMEM(slab, f32),
                pltpu.VMEM((4, half, rows, lanes), f32),
                pltpu.VMEM((4, half, rows, lanes), f32),
                pltpu.VMEM((3, *slab), f32),
                pltpu.VMEM((4, *slab), f32),
                pltpu.VMEM((4, *slab), f32),
                pltpu.VMEM(slab, f32),
                pltpu.VMEM(slab, f32),
                pltpu.VMEM((depth * rows, 2 * lanes), f32),
                pltpu.VMEM((3 * rows, 3 * rows), jnp.bfloat16),
                pltpu.VMEM((3 * lanes, 3 * lanes), jnp.bfloat16),
                pltpu.VMEM((depth * rows, lanes), f32),
                pltpu.VMEM((shots, chunk, lanes), f32),
                pltpu.VMEM((chunk, lanes), f32),
                pltpu.VMEM((length, wide, lanes), f32),
                pltpu.VMEM((3, wide, lanes), f32),
                pltpu.SemaphoreType.DMA((6,)),
                pltpu.SemaphoreType.DMA((2, 5)),
                pltpu.SemaphoreType.DMA((2, 5)),
                pltpu.SemaphoreType.DMA((2,)),
                pltpu.SemaphoreType.DMA((2,)),
                pltpu.SemaphoreType.DMA((3,)),
                pltpu.SemaphoreType.DMA((3,)),
                pltpu.SemaphoreType.REGULAR,
                pltpu.SemaphoreType.REGULAR((3,)),
            ],
            compiler_params=pltpu.CompilerParams(
                collective_id=0, has_side_effects=True, vmem_limit_bytes=54800 * 1024
            ),
            name="window",
        )(
            stiffness, buoyancy, forward_now, forward_prior, adjoint_now, adjoint_after,
            source_cells, wavelet, receiver_cells, residuals,
        ).reshape(slab)

    placed = (
        P("dom", None, None),
        P("dom", None, None),
        P("shot", "dom", None, None),
        P("shot", "dom", None, None),
        P("shot", "dom", None, None),
        P("shot", "dom", None, None),
        P("shot"),
        P("shot", None),
        P("shot", None),
        P("shot", None, None),
    )
    return jax.shard_map(
        shards, mesh=mesh, in_specs=placed, out_specs=P("dom", None, None), check_vma=False
    )
```

time: 49.8 us -> 41.1 us (0.83)
  the two profiles are of different devices: /device:TPU:497 before, /device:TPU:418 now
where the time goes in v2:
time: 41.1 us; the launch traced here: 41 us
  Pallas kernels  38.9 us (95%)
  between operations  1.36 us (3%)
  local copies, waits for them, and re-layouts  0.71 us (2%)
    pallas_call x1, Pallas kernels, shards(): pl.pallas_call(make_kernel(shots, doms, depth, rows, lanes, receivers), o...  38.9 us

profile of v2, /device:TPU:418, one launch (start us, length us, event | category | flops | bytes accessed | tf_op | source)
XLA Modules:
  0.0 41.0 jit_solution(11739548158298927333)
XLA Ops:
  0.0 0.0 copy-start
  0.7 0.0 copy-start.1
  1.3 0.0 copy-done
  1.3 0.0 copy-done.1
  1.4 38.9 %window.1 = f32[512,128]{1,0:T(8,128)S(1)} custom-call(f32[8,64,128]{2,1,0:T(8,128)} %stiff_hbm.1, f32[8,64,128]{2,1,0:T(8,128)} %buoy_hbm.1, f32[1,8,64,128]{3,2,1,0:T(8,128)} %now_hbm.1, f32[1,8,64,128]{3,2,1,0:T(8,128)} %prior_hbm.1, f32[1,8,64,128]{3,2,1,0:T(8,128)} %adj_hbm.1, f32[1,8,64,128]{3,2,1,0:T(8,128)} %after_hbm.1, s32[1]{0:T(128)S(6)} %copy.12.source_ref, ...), custom_call_target="tpu_custom_call" | custom-call | tf_op jit(solution)/shard_map/window/pallas_call | solution.py:543
  40.2 0.7 %copy.14 = f32[8,64,128]{2,1,0:T(8,128)} copy(f32[8,64,128]{2,1,0:T(8,128)S(1)} %bitcast.1) | data formatting | bytes 524288
Async XLA Ops:
  0.0 1.3 %copy-start = (f32[1,2,256]{2,1,0:T(2,128)S(1)}, f32[1,2,256]{2,1,0:T(2,128)}, u32[]{:S(2)}) copy-start(f32[1,2,256]{2,1,0:T(2,128)} %traces_ref.1) | copy-start | bytes 6148
  0.7 0.7 %copy-start.1 = (s32[1,256]{1,0:T(1,128)S(1)}, s32[1,256]{1,0:T(1,128)}, u32[]{:S(2)}) copy-start(s32[1,256]{1,0:T(1,128)} %cells_ref.1) | copy-start | bytes 3076

commit v3 on v2

--- a/solution.py
+++ b/solution.py
@@ -18,6 +18,7 @@
     length = shots // 2
     chunk = half * rows // shots
     wide = half * rows // length
+    band = rows // 2
     steps = sorted({1, length - 1})
     leaps = sorted({2 % length, (length - 2) % length} - {0})
 
@@ -55,8 +56,10 @@
         wide_parts,
         wide_sums,
         load_sem,
-        halo_send,
-        halo_recv,
+        far_send,
+        far_recv,
+        near_send,
+        near_recv,
         outer_send,
         outer_recv,
         inner_send,
@@ -175,8 +178,6 @@
                     last, low.astype(jnp.float32), high.astype(jnp.float32)
                 ).astype(jnp.bfloat16)
 
-        make_matrices()
-
         def dot(a, b):
             return lax.dot_general(
                 a, b, (((1,), (0,)), ((), ())), preferred_element_type=jnp.float32
@@ -198,35 +199,29 @@
             along_x = dot(left[use], stacked)
             return along_x, along_y
 
-        loads[2].wait()
-        loads[3].wait()
-
         def scale(z, carry):
             fields[SQ_NOW, WIDTH + z] = stiff[z] * adj[z]
             return carry
 
-        lax.fori_loop(0, depth, scale, 0)
-        loads[0].wait()
-        loads[1].wait()
-
-        def far_copy(f):
-            if f == 4:
-                src = buoy.at[pl.ds(WIDTH + outer, half)]
-                dst = buoy.at[pl.ds((1 - core) * (WIDTH + depth), half)]
-            else:
-                src = fields.at[f, pl.ds(WIDTH + outer, half)]
-                dst = far_halo.at[f]
-            return pltpu.make_async_remote_copy(
-                src, dst, halo_send.at[0, f], halo_recv.at[0, f], device_id={"dom": far}, device_id_type=MESH
-            )
-
-        def far_arrival(f):
-            if f == 4:
-                dst = buoy.at[pl.ds(core * (WIDTH + depth), half)]
-            else:
-                dst = far_halo.at[f]
-            return pltpu.make_async_remote_copy(
-                dst, dst, halo_send.at[0, f], halo_recv.at[0, f], device_id={"dom": far}, device_id_type=MESH
+        def far_ends(f, part, sending):
+            of = pl.ds(part * band, band)
+            if f < 4:
+                return far_halo.at[f, pl.ds(0, half), of]
+            at = 1 - core if sending else core
+            return buoy.at[pl.ds(at * (WIDTH + depth), half), of]
+
+        def far_copy(f, part):
+            src = (buoy if f == 4 else fields.at[f]).at[pl.ds(WIDTH + outer, half), pl.ds(part * band, band)]
+            return pltpu.make_async_remote_copy(
+                src, far_ends(f, part, True), far_send.at[f, part], far_recv.at[f, part],
+                device_id={"dom": far}, device_id_type=MESH,
+            )
+
+        def far_arrival(f, part):
+            dst = far_ends(f, part, False)
+            return pltpu.make_async_remote_copy(
+                dst, dst, far_send.at[f, part], far_recv.at[f, part],
+                device_id={"dom": far}, device_id_type=MESH,
             )
 
         def near_copy(f):
@@ -237,7 +232,7 @@
                 src = fields.at[f, pl.ds(WIDTH + inner, half)]
                 dst = near_halo.at[f]
             return pltpu.make_async_remote_copy(
-                src, dst, halo_send.at[1, f], halo_recv.at[1, f], device_id={"dom": near}, device_id_type=MESH
+                src, dst, near_send.at[f], near_recv.at[f], device_id={"dom": near}, device_id_type=MESH
             )
 
         def near_arrival(f):
@@ -246,7 +241,7 @@
             else:
                 dst = near_halo.at[f]
             return pltpu.make_async_remote_copy(
-                dst, dst, halo_send.at[1, f], halo_recv.at[1, f], device_id={"dom": near}, device_id_type=MESH
+                dst, dst, near_send.at[f], near_recv.at[f], device_id={"dom": near}, device_id_type=MESH
             )
 
         def when_far(act):
@@ -259,15 +254,15 @@
                     slopes[0, z + i] = along_x[:, i * lanes : (i + 1) * lanes]
                     slopes[1, z + i] = along_y[i * rows : (i + 1) * rows]
 
-        def buoy_slope_z(start):
+        def buoy_slope_z(start, use):
             def body(j, carry):
                 z = start + j
-                along_z = jnp.zeros((rows, lanes), jnp.float32)
+                along_z = jnp.zeros((use.size, lanes), jnp.float32)
                 for k in range(1, 5):
-                    up = buoy[WIDTH + z + k]
-                    down = buoy[WIDTH + z - k]
+                    up = buoy[WIDTH + z + k, use]
+                    down = buoy[WIDTH + z - k, use]
                     along_z = along_z + C_FIRST[k - 1] * (up - down)
-                slopes[2, z] = along_z
+                slopes[2, z, use] = along_z
                 return carry
 
             lax.fori_loop(0, half, body, 0)
@@ -293,13 +288,18 @@
                         + along_y[of_y, lanes : 2 * lanes] * slopes[1, z]
                     )
 
-        buoy_slopes()
-        local(P_NOW)
-        local(SQ_NOW)
+        loads[0].wait()
+        loads[1].wait()
         pl.semaphore_wait(barrier, len(steps) + 1 + far_count + (1 - core))
 
-        for f in (4, P_NOW, SQ_NOW):
-            when_far(far_copy(f).start)
+        for part in range(2):
+            for f in (4, P_NOW):
+                when_far(far_copy(f, part).start)
+        loads[2].wait()
+        loads[3].wait()
+        lax.fori_loop(0, depth, scale, 0)
+        for part in range(2):
+            when_far(far_copy(SQ_NOW, part).start)
 
         def near_begin():
             @pl.when(core == 0)
@@ -316,6 +316,11 @@
         pl.when(dom != 1)(near_begin)
         for i in steps:
             pl.semaphore_signal(greeted.at[0], 1, device_id=along(i), device_id_type=MESH)
+
+        make_matrices()
+        buoy_slopes()
+        local(P_NOW)
+        local(SQ_NOW)
 
         @pl.when(jnp.logical_not(has_far))
         def _():
@@ -325,52 +330,57 @@
                 for f in range(4):
                     far_halo[f, z] = blank
 
-        def whole(f, j, is_far):
+        def whole(f, j, is_far, use):
             halo = far_halo if is_far else near_halo
             up = core if is_far else 1 - core
             z = up * (depth - 1 - j) + (1 - up) * j
-            curve = jnp.zeros((rows, lanes), jnp.float32)
-            along = jnp.zeros((rows, lanes), jnp.float32)
+            curve = jnp.zeros((use.size, lanes), jnp.float32)
+            along = jnp.zeros((use.size, lanes), jnp.float32)
             for k in range(j + 1, 5):
                 m = k - j
                 plane_at = up * (m - 1) + (1 - up) * (half - m)
-                value = halo[f, plane_at]
+                value = halo[f, plane_at, use]
                 curve = curve + C_SECOND[k] * value
                 along = along + C_FIRST[k - 1] * value
             sign = side if is_far else -side
-            along = slope_z[f, z] + sign * along
-            return z, base[f, z] + buoy[WIDTH + z] * curve + along * slopes[2, z]
+            along = slope_z[f, z, use] + sign * along
+            value = base[f, z, use] + buoy[WIDTH + z, use] * curve + along * slopes[2, z, use]
+            return z, value
 
         for load in loads[4:]:
             load.wait()
         local_source = source_ref[...].reshape(1, 1) - dom * (depth * plane)
         amplitude = wavelet_ref[...]
-        cell = lax.broadcasted_iota(jnp.int32, (rows, lanes), 0) * lanes
-        cell = cell + lax.broadcasted_iota(jnp.int32, (rows, lanes), 1)
-
-        def forward(is_far):
+        everything = pl.ds(0, rows)
+
+        def forward(is_far, use=everything):
+            cell = lax.broadcasted_iota(jnp.int32, (use.size, lanes), 0) * lanes
+            cell = cell + lax.broadcasted_iota(jnp.int32, (use.size, lanes), 1)
             for j in range(half):
-                z, value = whole(P_NOW, j, is_far)
-                image[z] = value
-                shown = jnp.where(cell + z * plane == local_source, amplitude, 0.0)
-                fields[P_NEXT, WIDTH + z] = (
-                    2.0 * fields[P_NOW, WIDTH + z] - prior[z] + stiff[z] * value + shown
+                z, value = whole(P_NOW, j, is_far, use)
+                image[z, use] = value
+                here = cell + (z * plane + use.start * lanes)
+                shown = jnp.where(here == local_source, amplitude, 0.0)
+                fields[P_NEXT, WIDTH + z, use] = (
+                    2.0 * fields[P_NOW, WIDTH + z, use] - prior[z, use] + stiff[z, use] * value + shown
                 )
 
-        def backward(is_far):
+        def backward(is_far, use=everything):
             for j in range(half):
-                z, value = whole(SQ_NOW, j, is_far)
-                value = 2.0 * adj[z] - after[z] + value + injected[pl.ds(z * rows, rows), 0:lanes]
-                adj_next[z] = value
-                fields[SQ_NEXT, WIDTH + z] = stiff[z] * value
-
-        def finish(is_far):
+                z, value = whole(SQ_NOW, j, is_far, use)
+                injected_rows = pl.ds(z * rows + use.start, use.size)
+                value = 2.0 * adj[z, use] - after[z, use] + value + injected[injected_rows, 0:lanes]
+                adj_next[z, use] = value
+                fields[SQ_NEXT, WIDTH + z, use] = stiff[z, use] * value
+
+        def finish(is_far, use=everything):
             for j in range(half):
-                z, last_image = whole(P_NEXT, j, is_far)
-                _, value = whole(SQ_NEXT, j, is_far)
-                newer = adj_next[z]
-                value = 2.0 * newer - adj[z] + value + injected[pl.ds(z * rows, rows), lanes : 2 * lanes]
-                grad[pl.ds(z * rows, rows)] = newer * last_image + value * image[z]
+                z, last_image = whole(P_NEXT, j, is_far, use)
+                _, value = whole(SQ_NEXT, j, is_far, use)
+                newer = adj_next[z, use]
+                flat = pl.ds(z * rows + use.start, use.size)
+                value = 2.0 * newer - adj[z, use] + value + injected[flat, lanes : 2 * lanes]
+                grad[flat] = newer * last_image + value * image[z, use]
 
         def inject():
             local_cells = cells_ref[...] - dom * (depth * plane)
@@ -387,18 +397,25 @@
             row_hot = jnp.where(row == cell_rows, 1.0, 0.0).astype(jnp.bfloat16)
             injected[...] = dot(row_hot, low) + dot(row_hot, middle) + dot(row_hot, high)
 
-        def share(of):
-            return pl.ds(outer * rows + of * chunk, chunk)
-
-        def outer_copy(stage, i):
-            peer = lax.rem(shot + i, shots)
+        def share(of_row, of_column):
+            at = of_column * chunk
+            return pl.ds((outer + at // band) * rows + of_row * band + lax.rem(at, band), chunk)
+
+        def outer_copy(stage, to_row, i):
+            to_column = lax.rem(column + i, length)
             if stage == 0:
-                src, dst = grad.at[share(peer)], parts.at[shot]
+                src, dst = grad.at[share(to_row, to_column)], parts.at[shot]
             else:
-                src, dst = sums, out_ref.at[share(shot)]
-            return pltpu.make_async_remote_copy(
-                src, dst, outer_send.at[stage], outer_recv.at[stage], device_id={"shot": peer}, device_id_type=MESH
-            )
+                src, dst = sums, out_ref.at[share(row, column)]
+            return pltpu.make_async_remote_copy(
+                src, dst, outer_send.at[stage], outer_recv.at[stage],
+                device_id={"shot": to_row * length + to_column}, device_id_type=MESH,
+            )
+
+        def outer_start(stage, to_row):
+            for i in line:
+                outer_copy(stage, to_row, i).start()
+            pl.when(row != to_row)(outer_copy(stage, to_row, 0).start)
 
         def outer_all(stage):
             every = parts.at[pl.ds(0, shots - 1)]
@@ -431,7 +448,7 @@
 
         def near_fold():
             near_arrival(4).wait_recv()
-            buoy_slope_z(inner)
+            buoy_slope_z(inner, everything)
             near_arrival(P_NOW).wait_recv()
             forward(False)
             near_copy(P_NEXT).start()
@@ -441,20 +458,23 @@
 
         inject()
 
-        when_far(far_arrival(4).wait_recv)
-        buoy_slope_z(outer)
-        when_far(far_arrival(P_NOW).wait_recv)
-        forward(True)
-        when_far(far_copy(P_NEXT).start)
+        for part in range(2):
+            use = pl.ds(part * band, band)
+            when_far(far_arrival(4, part).wait_recv)
+            buoy_slope_z(outer, use)
+            when_far(far_arrival(P_NOW, part).wait_recv)
+            forward(True, use)
+            when_far(far_copy(P_NEXT, part).start)
 
         pl.semaphore_wait(greeted.at[0], len(steps))
         for i in leaps:
             pl.semaphore_signal(greeted.at[1], 1, device_id=along(i), device_id_type=MESH)
         pl.when(dom != 1)(near_fold)
 
-        when_far(far_arrival(SQ_NOW).wait_recv)
-        backward(True)
-        when_far(far_copy(SQ_NEXT).start)
+        for part in range(2):
+            when_far(far_arrival(SQ_NOW, part).wait_recv)
+            backward(True, pl.ds(part * band, band))
+            when_far(far_copy(SQ_NEXT, part).start)
 
         @pl.when(dom == 1)
         def _():
@@ -474,11 +494,11 @@
             inner_copy(0, i).start()
         pl.semaphore_wait(greeted.at[2], 1)
 
-        when_far(far_arrival(P_NEXT).wait_recv)
-        when_far(far_arrival(SQ_NEXT).wait_recv)
-        finish(True)
-        for i in peers:
-            outer_copy(0, i).start()
+        for part in range(2):
+            when_far(far_arrival(P_NEXT, part).wait_recv)
+            when_far(far_arrival(SQ_NEXT, part).wait_recv)
+            finish(True, pl.ds(part * band, band))
+            outer_start(0, part)
 
         inner_all(0).wait_recv()
         total = grad[wide_share(column)]
@@ -493,16 +513,17 @@
         out_ref[wide_share(column)] = wide_sums[2]
 
         outer_all(0).wait_recv()
-        total = grad[share(shot)]
+        total = grad[share(row, column)]
         for i in peers:
             total = total + parts[lax.rem(shot + i, shots)]
         sums[...] = total
-        for i in peers:
-            outer_copy(1, i).start()
-        out_ref[share(shot)] = total
+        for to_row in range(2):
+            outer_start(1, to_row)
+        out_ref[share(row, column)] = total
 
         for f in range(5):
-            when_far(far_copy(f).wait_send)
+            for part in range(2):
+                when_far(far_copy(f, part).wait_send)
             near_copy(f).wait_send()
         swap.wait_send()
         for stage in range(2):
@@ -568,8 +589,10 @@
                 pltpu.VMEM((length, wide, lanes), f32),
                 pltpu.VMEM((3, wide, lanes), f32),
                 pltpu.SemaphoreType.DMA((6,)),
-                pltpu.SemaphoreType.DMA((2, 5)),
-                pltpu.SemaphoreType.DMA((2, 5)),
+                pltpu.SemaphoreType.DMA((5, 2)),
+                pltpu.SemaphoreType.DMA((5, 2)),
+                pltpu.SemaphoreType.DMA((5,)),
+                pltpu.SemaphoreType.DMA((5,)),
                 pltpu.SemaphoreType.DMA((2,)),
                 pltpu.SemaphoreType.DMA((2,)),
                 pltpu.SemaphoreType.DMA((3,)),

time: 41.1 us -> 39.6 us (0.964)
  the two profiles are of different devices: /device:TPU:418 before, /device:TPU:417 now
where the time goes in v3:
time: 39.6 us; the launch traced here: 39.4 us
  Pallas kernels  37.4 us (94%)
  between operations  1.36 us (3%)
  local copies, waits for them, and re-layouts  0.71 us (2%)
    pallas_call x1, Pallas kernels, shards(): pl.pallas_call(make_kernel(shots, doms, depth, rows, lanes, receivers), o...  37.4 us

profile of v3, /device:TPU:417, one launch (start us, length us, event | category | flops | bytes accessed | tf_op | source)
XLA Modules:
  0.0 39.4 jit_solution(9586329037398590631)
XLA Ops:
  0.0 0.0 copy-start
  0.7 0.0 copy-start.1
  1.3 0.0 copy-done
  1.3 0.0 copy-done.1
  1.4 37.4 %window.1 = f32[512,128]{1,0:T(8,128)S(1)} custom-call(f32[8,64,128]{2,1,0:T(8,128)} %stiff_hbm.1, f32[8,64,128]{2,1,0:T(8,128)} %buoy_hbm.1, f32[1,8,64,128]{3,2,1,0:T(8,128)} %now_hbm.1, f32[1,8,64,128]{3,2,1,0:T(8,128)} %prior_hbm.1, f32[1,8,64,128]{3,2,1,0:T(8,128)} %adj_hbm.1, f32[1,8,64,128]{3,2,1,0:T(8,128)} %after_hbm.1, s32[1]{0:T(128)S(6)} %copy.12.source_ref, ...), custom_call_target="tpu_custom_call" | custom-call | tf_op jit(solution)/shard_map/window/pallas_call | solution.py:564
  38.7 0.7 %copy.14 = f32[8,64,128]{2,1,0:T(8,128)} copy(f32[8,64,128]{2,1,0:T(8,128)S(1)} %bitcast.1) | data formatting | bytes 524288
Async XLA Ops:
  0.0 1.3 %copy-start = (f32[1,2,256]{2,1,0:T(2,128)S(1)}, f32[1,2,256]{2,1,0:T(2,128)}, u32[]{:S(2)}) copy-start(f32[1,2,256]{2,1,0:T(2,128)} %traces_ref.1) | copy-start | bytes 6148
  0.7 0.7 %copy-start.1 = (s32[1,256]{1,0:T(1,128)S(1)}, s32[1,256]{1,0:T(1,128)}, u32[]{:S(2)}) copy-start(s32[1,256]{1,0:T(1,128)} %cells_ref.1) | copy-start | bytes 3076

commit v4 on v3

--- a/solution.py
+++ b/solution.py
@@ -19,6 +19,10 @@
     chunk = half * rows // shots
     wide = half * rows // length
     band = rows // 2
+
+    def band_rows(part):
+        return pl.ds(pl.multiple_of(part * band, band), band)
+
     steps = sorted({1, length - 1})
     leaps = sorted({2 % length, (length - 2) % length} - {0})
 
@@ -53,18 +57,20 @@
         grad,
         parts,
         sums,
-        wide_parts,
-        wide_sums,
         load_sem,
         far_send,
         far_recv,
         near_send,
         near_recv,
-        outer_send,
-        outer_recv,
-        inner_send,
-        inner_recv,
+        share_send,
+        share_recv,
+        wide_parts,
+        wide_sums,
+        wide_send,
+        wide_recv,
         near_ready,
+        pass_send,
+        pass_recv,
         greeted,
     ):
         shot = lax.axis_index("shot")
@@ -84,7 +90,6 @@
             return {"shot": row * length + lax.rem(column + i, length)}
 
         across = {"shot": (1 - row) * length + column}
-        peers = sorted(range(1, shots), key=lambda i: -min(i % length, length - i % length))
         line = sorted(range(1, length), key=lambda i: -min(i, length - i))
 
         barrier = pltpu.get_barrier_semaphore()
@@ -199,19 +204,36 @@
             along_x = dot(left[use], stacked)
             return along_x, along_y
 
+        def inject():
+            local_cells = cells_ref[...] - dom * (depth * plane)
+            cell_rows = jnp.right_shift(local_cells, 7)
+            cell_lanes = jnp.bitwise_and(local_cells, lanes - 1)
+            lane_hot = lax.broadcasted_iota(jnp.int32, (lanes, receivers), 0) == cell_lanes
+            amounts = jnp.concatenate(
+                [jnp.where(lane_hot, traces_ref[0, k : k + 1, :], 0.0) for k in range(2)], axis=0
+            )
+            amounts = amounts.T
+            high, _ = split(amounts)
+            middle, low = split(amounts - high.astype(jnp.float32))
+            row = lax.broadcasted_iota(jnp.int32, (depth * rows, receivers), 0)
+            row_hot = jnp.where(row == cell_rows, 1.0, 0.0).astype(jnp.bfloat16)
+            injected[...] = dot(row_hot, low) + dot(row_hot, middle) + dot(row_hot, high)
+
         def scale(z, carry):
             fields[SQ_NOW, WIDTH + z] = stiff[z] * adj[z]
             return carry
 
+        bands = [lax.rem(column + i, 2) for i in range(2)]
+
         def far_ends(f, part, sending):
-            of = pl.ds(part * band, band)
+            of = band_rows(part)
             if f < 4:
                 return far_halo.at[f, pl.ds(0, half), of]
             at = 1 - core if sending else core
             return buoy.at[pl.ds(at * (WIDTH + depth), half), of]
 
         def far_copy(f, part):
-            src = (buoy if f == 4 else fields.at[f]).at[pl.ds(WIDTH + outer, half), pl.ds(part * band, band)]
+            src = (buoy if f == 4 else fields.at[f]).at[pl.ds(WIDTH + outer, half), band_rows(part)]
             return pltpu.make_async_remote_copy(
                 src, far_ends(f, part, True), far_send.at[f, part], far_recv.at[f, part],
                 device_id={"dom": far}, device_id_type=MESH,
@@ -222,6 +244,13 @@
             return pltpu.make_async_remote_copy(
                 dst, dst, far_send.at[f, part], far_recv.at[f, part],
                 device_id={"dom": far}, device_id_type=MESH,
+            )
+
+        def pass_on(part):
+            ends = far_ends(4, part, False)
+            return pltpu.make_async_remote_copy(
+                ends, ends, pass_send, pass_recv,
+                device_id={"shot": row * length + column + 1 - 2 * lax.rem(column, 2)}, device_id_type=MESH,
             )
 
         def near_copy(f):
@@ -288,17 +317,19 @@
                         + along_y[of_y, lanes : 2 * lanes] * slopes[1, z]
                     )
 
+        make_matrices()
+        inject()
         loads[0].wait()
         loads[1].wait()
         pl.semaphore_wait(barrier, len(steps) + 1 + far_count + (1 - core))
 
-        for part in range(2):
-            for f in (4, P_NOW):
-                when_far(far_copy(f, part).start)
+        when_far(far_copy(4, bands[0]).start)
+        for part in bands:
+            when_far(far_copy(P_NOW, part).start)
         loads[2].wait()
         loads[3].wait()
         lax.fori_loop(0, depth, scale, 0)
-        for part in range(2):
+        for part in bands:
             when_far(far_copy(SQ_NOW, part).start)
 
         def near_begin():
@@ -317,7 +348,6 @@
         for i in steps:
             pl.semaphore_signal(greeted.at[0], 1, device_id=along(i), device_id_type=MESH)
 
-        make_matrices()
         buoy_slopes()
         local(P_NOW)
         local(SQ_NOW)
@@ -353,6 +383,9 @@
         amplitude = wavelet_ref[...]
         everything = pl.ds(0, rows)
 
+        def flat_rows(z, use):
+            return pl.ds(pl.multiple_of(z * rows + use.start, band), use.size)
+
         def forward(is_far, use=everything):
             cell = lax.broadcasted_iota(jnp.int32, (use.size, lanes), 0) * lanes
             cell = cell + lax.broadcasted_iota(jnp.int32, (use.size, lanes), 1)
@@ -368,7 +401,7 @@
         def backward(is_far, use=everything):
             for j in range(half):
                 z, value = whole(SQ_NOW, j, is_far, use)
-                injected_rows = pl.ds(z * rows + use.start, use.size)
+                injected_rows = flat_rows(z, use)
                 value = 2.0 * adj[z, use] - after[z, use] + value + injected[injected_rows, 0:lanes]
                 adj_next[z, use] = value
                 fields[SQ_NEXT, WIDTH + z, use] = stiff[z, use] * value
@@ -378,73 +411,85 @@
                 z, last_image = whole(P_NEXT, j, is_far, use)
                 _, value = whole(SQ_NEXT, j, is_far, use)
                 newer = adj_next[z, use]
-                flat = pl.ds(z * rows + use.start, use.size)
+                flat = flat_rows(z, use)
                 value = 2.0 * newer - adj[z, use] + value + injected[flat, lanes : 2 * lanes]
                 grad[flat] = newer * last_image + value * image[z, use]
 
-        def inject():
-            local_cells = cells_ref[...] - dom * (depth * plane)
-            cell_rows = jnp.right_shift(local_cells, 7)
-            cell_lanes = jnp.bitwise_and(local_cells, lanes - 1)
-            lane_hot = lax.broadcasted_iota(jnp.int32, (lanes, receivers), 0) == cell_lanes
-            amounts = jnp.concatenate(
-                [jnp.where(lane_hot, traces_ref[0, k : k + 1, :], 0.0) for k in range(2)], axis=0
-            )
-            amounts = amounts.T
-            high, _ = split(amounts)
-            middle, low = split(amounts - high.astype(jnp.float32))
-            row = lax.broadcasted_iota(jnp.int32, (depth * rows, receivers), 0)
-            row_hot = jnp.where(row == cell_rows, 1.0, 0.0).astype(jnp.bfloat16)
-            injected[...] = dot(row_hot, low) + dot(row_hot, middle) + dot(row_hot, high)
-
-        def share(of_row, of_column):
+        def share(h, of_row, of_column):
+            if h == 0:
+                return pl.ds(inner * rows + (of_row * length + of_column) * chunk, chunk)
             at = of_column * chunk
             return pl.ds((outer + at // band) * rows + of_row * band + lax.rem(at, band), chunk)
 
-        def outer_copy(stage, to_row, i):
+        def share_copy(h, stage, to_row, i):
             to_column = lax.rem(column + i, length)
             if stage == 0:
-                src, dst = grad.at[share(to_row, to_column)], parts.at[shot]
+                src, dst = grad.at[share(h, to_row, to_column)], parts.at[h, shot]
             else:
-                src, dst = sums, out_ref.at[share(row, column)]
-            return pltpu.make_async_remote_copy(
-                src, dst, outer_send.at[stage], outer_recv.at[stage],
+                src, dst = sums.at[h], out_ref.at[share(h, row, column)]
+            return pltpu.make_async_remote_copy(
+                src, dst, share_send.at[h, stage], share_recv.at[h, stage],
                 device_id={"shot": to_row * length + to_column}, device_id_type=MESH,
             )
 
-        def outer_start(stage, to_row):
+        def share_start(h, stage, to_row):
             for i in line:
-                outer_copy(stage, to_row, i).start()
-            pl.when(row != to_row)(outer_copy(stage, to_row, 0).start)
-
-        def outer_all(stage):
-            every = parts.at[pl.ds(0, shots - 1)]
-            return pltpu.make_async_remote_copy(
-                every, every, outer_send.at[stage], outer_recv.at[stage], device_id=across, device_id_type=MESH
-            )
+                share_copy(h, stage, to_row, i).start()
+            pl.when(row != to_row)(share_copy(h, stage, to_row, 0).start)
+
+        def all_shares(h, stage):
+            every = parts.at[h, pl.ds(0, shots - 1)]
+            return pltpu.make_async_remote_copy(
+                every, every, share_send.at[h, stage], share_recv.at[h, stage], device_id=across, device_id_type=MESH
+            )
+
+        def add_shares(h):
+            all_shares(h, 0).wait_recv()
+            total = grad[share(h, row, column)]
+            for i in range(1, shots):
+                total = total + parts[h, lax.rem(shot + i, shots)]
+            sums[h] = total
+            for to_row in range(2):
+                share_start(h, 1, to_row)
+            out_ref[share(h, row, column)] = total
 
         def wide_share(of):
             return pl.ds(inner * rows + of * wide, wide)
 
-        def inner_copy(stage, i):
+        def wide_copy(stage, i):
             peer = lax.rem(column + i, length)
             if stage == 0:
                 src, dst = grad.at[wide_share(peer)], wide_parts.at[column]
             else:
                 src, dst = wide_sums.at[2], out_ref.at[wide_share(column)]
             return pltpu.make_async_remote_copy(
-                src, dst, inner_send.at[stage], inner_recv.at[stage], device_id=along(i), device_id_type=MESH
-            )
-
-        def inner_all(stage):
+                src, dst, wide_send.at[stage], wide_recv.at[stage], device_id=along(i), device_id_type=MESH
+            )
+
+        def all_wide(stage):
             every = wide_parts.at[pl.ds(0, length - 1)]
             return pltpu.make_async_remote_copy(
-                every, every, inner_send.at[stage], inner_recv.at[stage], device_id=across, device_id_type=MESH
+                every, every, wide_send.at[stage], wide_recv.at[stage], device_id=across, device_id_type=MESH
             )
 
         swap = pltpu.make_async_remote_copy(
-            wide_sums.at[0], wide_sums.at[1], inner_send.at[2], inner_recv.at[2], device_id=across, device_id_type=MESH
+            wide_sums.at[0], wide_sums.at[1], wide_send.at[2], wide_recv.at[2], device_id=across, device_id_type=MESH
         )
+
+        def add_wide():
+            all_wide(0).wait_recv()
+            total = grad[wide_share(column)]
+            for i in line:
+                total = total + wide_parts[lax.rem(column + i, length)]
+            wide_sums[0] = total
+            swap.start()
+            swap.wait_recv()
+            wide_sums[2] = wide_sums[0] + wide_sums[1]
+            for i in line:
+                wide_copy(1, i).start()
+            out_ref[wide_share(column)] = wide_sums[2]
+
+        direct = dom < 2
 
         def near_fold():
             near_arrival(4).wait_recv()
@@ -456,11 +501,12 @@
             backward(False)
             near_copy(SQ_NEXT).start()
 
-        inject()
-
-        for part in range(2):
-            use = pl.ds(part * band, band)
-            when_far(far_arrival(4, part).wait_recv)
+        when_far(far_arrival(4, bands[0]).wait_recv)
+        when_far(pass_on(bands[0]).start)
+        for part in bands:
+            use = band_rows(part)
+            if part is bands[1]:
+                when_far(pass_on(part).wait_recv)
             buoy_slope_z(outer, use)
             when_far(far_arrival(P_NOW, part).wait_recv)
             forward(True, use)
@@ -471,9 +517,9 @@
             pl.semaphore_signal(greeted.at[1], 1, device_id=along(i), device_id_type=MESH)
         pl.when(dom != 1)(near_fold)
 
-        for part in range(2):
+        for part in bands:
             when_far(far_arrival(SQ_NOW, part).wait_recv)
-            backward(True, pl.ds(part * band, band))
+            backward(True, band_rows(part))
             when_far(far_copy(SQ_NEXT, part).start)
 
         @pl.when(dom == 1)
@@ -490,48 +536,54 @@
         near_arrival(P_NEXT).wait_recv()
         near_arrival(SQ_NEXT).wait_recv()
         finish(False)
-        for i in line:
-            inner_copy(0, i).start()
         pl.semaphore_wait(greeted.at[2], 1)
 
-        for part in range(2):
+        @pl.when(direct)
+        def _():
+            for to_row in range(2):
+                share_start(0, 0, to_row)
+
+        @pl.when(jnp.logical_not(direct))
+        def _():
+            for i in line:
+                wide_copy(0, i).start()
+
+
+        for part in bands:
             when_far(far_arrival(P_NEXT, part).wait_recv)
             when_far(far_arrival(SQ_NEXT, part).wait_recv)
-            finish(True, pl.ds(part * band, band))
-            outer_start(0, part)
-
-        inner_all(0).wait_recv()
-        total = grad[wide_share(column)]
-        for i in line:
-            total = total + wide_parts[lax.rem(column + i, length)]
-        wide_sums[0] = total
-        swap.start()
-        swap.wait_recv()
-        wide_sums[2] = wide_sums[0] + wide_sums[1]
-        for i in line:
-            inner_copy(1, i).start()
-        out_ref[wide_share(column)] = wide_sums[2]
-
-        outer_all(0).wait_recv()
-        total = grad[share(row, column)]
-        for i in peers:
-            total = total + parts[lax.rem(shot + i, shots)]
-        sums[...] = total
-        for to_row in range(2):
-            outer_start(1, to_row)
-        out_ref[share(row, column)] = total
+            finish(True, band_rows(part))
+            share_start(1, 0, part)
+
+        @pl.when(direct)
+        def _():
+            add_shares(0)
+
+        pl.when(jnp.logical_not(direct))(add_wide)
+        add_shares(1)
 
         for f in range(5):
-            for part in range(2):
+            for part in bands[: 1 if f == 4 else 2]:
                 when_far(far_copy(f, part).wait_send)
             near_copy(f).wait_send()
-        swap.wait_send()
-        for stage in range(2):
-            inner_all(stage).wait_send()
-        outer_all(0).wait_send()
-        inner_all(1).wait_recv()
-        outer_all(1).wait_send()
-        outer_all(1).wait_recv()
+        when_far(pass_on(bands[0]).wait_send)
+        def drain(h):
+            for stage in range(2):
+                all_shares(h, stage).wait_send()
+            all_shares(h, 1).wait_recv()
+
+        @pl.when(direct)
+        def _():
+            drain(0)
+
+        @pl.when(jnp.logical_not(direct))
+        def _():
+            for stage in range(2):
+                all_wide(stage).wait_send()
+            swap.wait_send()
+            all_wide(1).wait_recv()
+
+        drain(1)
 
     return kernel
 
@@ -554,9 +606,8 @@
         depth, rows, lanes = stiffness.shape
         receivers = receiver_cells.shape[1]
         half = depth // 2
-        length = shots // 2
         chunk = half * rows // shots
-        wide = half * rows // length
+        wide = 2 * chunk
         padded = (depth + 2 * WIDTH, rows, lanes)
         slab = (depth, rows, lanes)
         f32 = jnp.float32
@@ -584,20 +635,22 @@
                 pltpu.VMEM((3 * rows, 3 * rows), jnp.bfloat16),
                 pltpu.VMEM((3 * lanes, 3 * lanes), jnp.bfloat16),
                 pltpu.VMEM((depth * rows, lanes), f32),
-                pltpu.VMEM((shots, chunk, lanes), f32),
-                pltpu.VMEM((chunk, lanes), f32),
-                pltpu.VMEM((length, wide, lanes), f32),
-                pltpu.VMEM((3, wide, lanes), f32),
+                pltpu.VMEM((2, shots, chunk, lanes), f32),
+                pltpu.VMEM((2, chunk, lanes), f32),
                 pltpu.SemaphoreType.DMA((6,)),
                 pltpu.SemaphoreType.DMA((5, 2)),
                 pltpu.SemaphoreType.DMA((5, 2)),
                 pltpu.SemaphoreType.DMA((5,)),
                 pltpu.SemaphoreType.DMA((5,)),
-                pltpu.SemaphoreType.DMA((2,)),
-                pltpu.SemaphoreType.DMA((2,)),
+                pltpu.SemaphoreType.DMA((2, 2)),
+                pltpu.SemaphoreType.DMA((2, 2)),
+                pltpu.VMEM((shots // 2, wide, lanes), f32),
+                pltpu.VMEM((3, wide, lanes), f32),
                 pltpu.SemaphoreType.DMA((3,)),
                 pltpu.SemaphoreType.DMA((3,)),
                 pltpu.SemaphoreType.REGULAR,
+                pltpu.SemaphoreType.DMA,
+                pltpu.SemaphoreType.DMA,
                 pltpu.SemaphoreType.REGULAR((3,)),
             ],
             compiler_params=pltpu.CompilerParams(

time: 39.6 us -> 38.9 us (0.982)
  the two profiles are of different devices: /device:TPU:417 before, /device:TPU:32 now
where the time goes in v4:
time: 38.9 us; the launch traced here: 38.7 us
  Pallas kernels  36.6 us (94%)
  between operations  1.36 us (3%)
  local copies, waits for them, and re-layouts  0.71 us (2%)
    pallas_call x1, Pallas kernels, shards(): pl.pallas_call(make_kernel(shots, doms, depth, rows, lanes, receivers), o...  36.6 us

profile of v4, /device:TPU:32, one launch (start us, length us, event | category | flops | bytes accessed | tf_op | source)
XLA Modules:
  0.0 38.7 jit_solution(6421015985359373098)
XLA Ops:
  0.0 0.0 copy-start
  0.7 0.0 copy-start.1
  1.3 0.0 copy-done
  1.3 0.0 copy-done.1
  1.4 36.6 %window.1 = f32[512,128]{1,0:T(8,128)S(1)} custom-call(f32[8,64,128]{2,1,0:T(8,128)} %stiff_hbm.1, f32[8,64,128]{2,1,0:T(8,128)} %buoy_hbm.1, f32[1,8,64,128]{3,2,1,0:T(8,128)} %now_hbm.1, f32[1,8,64,128]{3,2,1,0:T(8,128)} %prior_hbm.1, f32[1,8,64,128]{3,2,1,0:T(8,128)} %adj_hbm.1, f32[1,8,64,128]{3,2,1,0:T(8,128)} %after_hbm.1, s32[1]{0:T(128)S(6)} %copy.12.source_ref, ...), custom_call_target="tpu_custom_call" | custom-call | tf_op jit(solution)/shard_map/window/pallas_call | solution.py:615
  38.0 0.7 %copy.14 = f32[8,64,128]{2,1,0:T(8,128)} copy(f32[8,64,128]{2,1,0:T(8,128)S(1)} %bitcast.1) | data formatting | bytes 524288
Async XLA Ops:
  0.0 1.3 %copy-start = (f32[1,2,256]{2,1,0:T(2,128)S(1)}, f32[1,2,256]{2,1,0:T(2,128)}, u32[]{:S(2)}) copy-start(f32[1,2,256]{2,1,0:T(2,128)} %traces_ref.1) | copy-start | bytes 6148
  0.7 0.7 %copy-start.1 = (s32[1,256]{1,0:T(1,128)S(1)}, s32[1,256]{1,0:T(1,128)}, u32[]{:S(2)}) copy-start(s32[1,256]{1,0:T(1,128)} %cells_ref.1) | copy-start | bytes 3076

commit v5 on v4

--- a/solution.py
+++ b/solution.py
@@ -33,11 +33,15 @@
         prior_hbm,
         adj_hbm,
         after_hbm,
+        source_any,
+        wavelet_any,
+        cells_any,
+        traces_any,
+        out_ref,
         source_ref,
         wavelet_ref,
         cells_ref,
         traces_ref,
-        out_ref,
         buoy,
         fields,
         stiff,
@@ -58,6 +62,7 @@
         parts,
         sums,
         load_sem,
+        own_sem,
         far_send,
         far_recv,
         near_send,
@@ -116,6 +121,10 @@
                     (adj_hbm.at[0], adj),
                     (prior_hbm.at[0], prior),
                     (after_hbm.at[0], after),
+                    (cells_any, cells_ref),
+                    (traces_any, traces_ref),
+                    (source_any, source_ref),
+                    (wavelet_any, wavelet_ref),
                 )
             )
         ]
@@ -318,7 +327,6 @@
                     )
 
         make_matrices()
-        inject()
         loads[0].wait()
         loads[1].wait()
         pl.semaphore_wait(barrier, len(steps) + 1 + far_count + (1 - core))
@@ -351,6 +359,9 @@
         buoy_slopes()
         local(P_NOW)
         local(SQ_NOW)
+        loads[6].wait()
+        loads[7].wait()
+        inject()
 
         @pl.when(jnp.logical_not(has_far))
         def _():
@@ -377,10 +388,10 @@
             value = base[f, z, use] + buoy[WIDTH + z, use] * curve + along * slopes[2, z, use]
             return z, value
 
-        for load in loads[4:]:
-            load.wait()
-        local_source = source_ref[...].reshape(1, 1) - dom * (depth * plane)
-        amplitude = wavelet_ref[...]
+        for i in (4, 5, 8, 9):
+            loads[i].wait()
+        local_source = source_ref[0] - dom * (depth * plane)
+        amplitude = wavelet_ref[0, 0]
         everything = pl.ds(0, rows)
 
         def flat_rows(z, use):
@@ -449,9 +460,13 @@
             for i in range(1, shots):
                 total = total + parts[h, lax.rem(shot + i, shots)]
             sums[h] = total
-            for to_row in range(2):
-                share_start(h, 1, to_row)
-            out_ref[share(h, row, column)] = total
+            share_copy(h, 1, 1 - row, length // 2).start()
+            for i in line:
+                share_copy(h, 1, row, i).start()
+                if i != length // 2:
+                    share_copy(h, 1, 1 - row, i).start()
+            share_copy(h, 1, 1 - row, 0).start()
+            pltpu.make_async_copy(sums.at[h], out_ref.at[share(h, row, column)], own_sem.at[h]).start()
 
         def wide_share(of):
             return pl.ds(inner * rows + of * wide, wide)
@@ -476,18 +491,20 @@
             wide_sums.at[0], wide_sums.at[1], wide_send.at[2], wide_recv.at[2], device_id=across, device_id_type=MESH
         )
 
-        def add_wide():
+        def swap_wide():
             all_wide(0).wait_recv()
             total = grad[wide_share(column)]
             for i in line:
                 total = total + wide_parts[lax.rem(column + i, length)]
             wide_sums[0] = total
             swap.start()
+
+        def add_wide():
             swap.wait_recv()
             wide_sums[2] = wide_sums[0] + wide_sums[1]
             for i in line:
                 wide_copy(1, i).start()
-            out_ref[wide_share(column)] = wide_sums[2]
+            pltpu.make_async_copy(wide_sums.at[2], out_ref.at[wide_share(column)], own_sem.at[2]).start()
 
         direct = dom < 2
 
@@ -501,8 +518,15 @@
             backward(False)
             near_copy(SQ_NEXT).start()
 
+        pl.when(dom != 1)(near_fold)
+        pl.semaphore_wait(greeted.at[0], len(steps))
+        for i in leaps:
+            pl.semaphore_signal(greeted.at[1], 1, device_id=along(i), device_id_type=MESH)
         when_far(far_arrival(4, bands[0]).wait_recv)
         when_far(pass_on(bands[0]).start)
+        if leaps:
+            pl.semaphore_wait(greeted.at[1], len(leaps))
+        pl.semaphore_signal(greeted.at[2], 1, device_id=across, device_id_type=MESH)
         for part in bands:
             use = band_rows(part)
             if part is bands[1]:
@@ -512,10 +536,7 @@
             forward(True, use)
             when_far(far_copy(P_NEXT, part).start)
 
-        pl.semaphore_wait(greeted.at[0], len(steps))
-        for i in leaps:
-            pl.semaphore_signal(greeted.at[1], 1, device_id=along(i), device_id_type=MESH)
-        pl.when(dom != 1)(near_fold)
+        pl.when(dom != 1)(lambda: local(P_NEXT))
 
         for part in bands:
             when_far(far_arrival(SQ_NOW, part).wait_recv)
@@ -526,16 +547,13 @@
         def _():
             near_begin()
             near_fold()
-
-        if leaps:
-            pl.semaphore_wait(greeted.at[1], len(leaps))
-        pl.semaphore_signal(greeted.at[2], 1, device_id=across, device_id_type=MESH)
-
-        local(P_NEXT)
+            local(P_NEXT)
+
         local(SQ_NEXT)
         near_arrival(P_NEXT).wait_recv()
         near_arrival(SQ_NEXT).wait_recv()
         finish(False)
+
         pl.semaphore_wait(greeted.at[2], 1)
 
         @pl.when(direct)
@@ -554,6 +572,8 @@
             when_far(far_arrival(SQ_NEXT, part).wait_recv)
             finish(True, band_rows(part))
             share_start(1, 0, part)
+            if part is bands[0]:
+                pl.when(jnp.logical_not(direct))(swap_wide)
 
         @pl.when(direct)
         def _():
@@ -570,6 +590,7 @@
         def drain(h):
             for stage in range(2):
                 all_shares(h, stage).wait_send()
+            pltpu.make_async_copy(sums.at[h], out_ref.at[share(h, row, column)], own_sem.at[h]).wait()
             all_shares(h, 1).wait_recv()
 
         @pl.when(direct)
@@ -581,6 +602,7 @@
             for stage in range(2):
                 all_wide(stage).wait_send()
             swap.wait_send()
+            pltpu.make_async_copy(wide_sums.at[2], out_ref.at[wide_share(column)], own_sem.at[2]).wait()
             all_wide(1).wait_recv()
 
         drain(1)
@@ -612,12 +634,17 @@
         slab = (depth, rows, lanes)
         f32 = jnp.float32
         in_hbm = pl.BlockSpec(memory_space=pltpu.HBM)
+        in_any = pl.BlockSpec(memory_space=pl.ANY)
         return pl.pallas_call(
             make_kernel(shots, doms, depth, rows, lanes, receivers),
             out_shape=jax.ShapeDtypeStruct((depth * rows, lanes), f32),
-            in_specs=[in_hbm] * 6 + [pl.BlockSpec(memory_space=pltpu.VMEM)] * 4,
-            out_specs=pl.BlockSpec(memory_space=pltpu.VMEM),
+            in_specs=[in_hbm] * 6 + [in_any] * 4,
+            out_specs=in_any,
             scratch_shapes=[
+                pltpu.SMEM((1,), jnp.int32),
+                pltpu.SMEM((1, 1), f32),
+                pltpu.VMEM((1, receivers), jnp.int32),
+                pltpu.VMEM((1, 2, receivers), f32),
                 pltpu.VMEM(padded, f32),
                 pltpu.VMEM((4, *padded), f32),
                 pltpu.VMEM(slab, f32),
@@ -637,7 +664,8 @@
                 pltpu.VMEM((depth * rows, lanes), f32),
                 pltpu.VMEM((2, shots, chunk, lanes), f32),
                 pltpu.VMEM((2, chunk, lanes), f32),
-                pltpu.SemaphoreType.DMA((6,)),
+                pltpu.SemaphoreType.DMA((10,)),
+                pltpu.SemaphoreType.DMA((3,)),
                 pltpu.SemaphoreType.DMA((5, 2)),
                 pltpu.SemaphoreType.DMA((5, 2)),
                 pltpu.SemaphoreType.DMA((5,)),

time: 38.9 us -> 38.3 us (0.985)
  the two profiles are of different devices: /device:TPU:32 before, /device:TPU:576 now
where the time goes in v5:
time: 38.3 us; the launch traced here: 38.1 us
  Pallas kernels  36 us (94%)
  between operations  1.36 us (4%)
  local copies, waits for them, and re-layouts  0.71 us (2%)
    pallas_call x1, Pallas kernels, shards(): pl.pallas_call(make_kernel(shots, doms, depth, rows, lanes, receivers), o...  36 us

profile of v5, /device:TPU:576, one launch (start us, length us, event | category | flops | bytes accessed | tf_op | source)
XLA Modules:
  0.0 38.1 jit_solution(12721225283031874646)
XLA Ops:
  0.0 0.0 copy-start
  0.7 0.0 copy-start.1
  1.3 0.0 copy-done
  1.3 0.0 copy-done.1
  1.4 36.0 %window.1 = f32[512,128]{1,0:T(8,128)S(1)} custom-call(f32[8,64,128]{2,1,0:T(8,128)} %stiff_hbm.1, f32[8,64,128]{2,1,0:T(8,128)} %buoy_hbm.1, f32[1,8,64,128]{3,2,1,0:T(8,128)} %now_hbm.1, f32[1,8,64,128]{3,2,1,0:T(8,128)} %prior_hbm.1, f32[1,8,64,128]{3,2,1,0:T(8,128)} %adj_hbm.1, f32[1,8,64,128]{3,2,1,0:T(8,128)} %after_hbm.1, s32[1]{0:T(128)S(6)} %copy.12.source_any, ...), custom_call_target="tpu_custom_call" | custom-call | tf_op jit(solution)/shard_map/window/pallas_call | solution.py:638
  37.4 0.7 %copy.14 = f32[8,64,128]{2,1,0:T(8,128)} copy(f32[8,64,128]{2,1,0:T(8,128)S(1)} %bitcast.1) | data formatting | bytes 524288
Async XLA Ops:
  0.0 1.3 %copy-start = (f32[1,2,256]{2,1,0:T(2,128)S(1)}, f32[1,2,256]{2,1,0:T(2,128)}, u32[]{:S(2)}) copy-start(f32[1,2,256]{2,1,0:T(2,128)} %traces_any.1) | copy-start | bytes 6148
  0.7 0.7 %copy-start.1 = (s32[1,256]{1,0:T(1,128)S(1)}, s32[1,256]{1,0:T(1,128)}, u32[]{:S(2)}) copy-start(s32[1,256]{1,0:T(1,128)} %cells_any.1) | copy-start | bytes 3076

commit v6 on v5

--- a/solution.py
+++ b/solution.py
@@ -502,7 +502,7 @@
         def add_wide():
             swap.wait_recv()
             wide_sums[2] = wide_sums[0] + wide_sums[1]
-            for i in line:
+            for i in reversed(line):
                 wide_copy(1, i).start()
             pltpu.make_async_copy(wide_sums.at[2], out_ref.at[wide_share(column)], own_sem.at[2]).start()
 
@@ -524,9 +524,6 @@
             pl.semaphore_signal(greeted.at[1], 1, device_id=along(i), device_id_type=MESH)
         when_far(far_arrival(4, bands[0]).wait_recv)
         when_far(pass_on(bands[0]).start)
-        if leaps:
-            pl.semaphore_wait(greeted.at[1], len(leaps))
-        pl.semaphore_signal(greeted.at[2], 1, device_id=across, device_id_type=MESH)
         for part in bands:
             use = band_rows(part)
             if part is bands[1]:
@@ -536,6 +533,9 @@
             forward(True, use)
             when_far(far_copy(P_NEXT, part).start)
 
+        if leaps:
+            pl.semaphore_wait(greeted.at[1], len(leaps))
+        pl.semaphore_signal(greeted.at[2], 1, device_id=across, device_id_type=MESH)
         pl.when(dom != 1)(lambda: local(P_NEXT))
 
         for part in bands:

time: 38.3 us -> 38.2 us (level)
  the two profiles are of different devices: /device:TPU:576 before, /device:TPU:289 now
where the time goes in v6:
time: 38.2 us; the launch traced here: 38 us
  Pallas kernels  35.9 us (94%)
  between operations  1.36 us (4%)
  local copies, waits for them, and re-layouts  0.71 us (2%)
    pallas_call x1, Pallas kernels, shards(): pl.pallas_call(make_kernel(shots, doms, depth, rows, lanes, receivers), o...  35.9 us

profile of v6, /device:TPU:289, one launch (start us, length us, event | category | flops | bytes accessed | tf_op | source)
XLA Modules:
  0.0 38.0 jit_solution(1907921558220193363)
XLA Ops:
  0.0 0.0 copy-start
  0.7 0.0 copy-start.1
  1.3 0.0 copy-done
  1.3 0.0 copy-done.1
  1.4 35.9 %window.1 = f32[512,128]{1,0:T(8,128)S(1)} custom-call(f32[8,64,128]{2,1,0:T(8,128)} %stiff_hbm.1, f32[8,64,128]{2,1,0:T(8,128)} %buoy_hbm.1, f32[1,8,64,128]{3,2,1,0:T(8,128)} %now_hbm.1, f32[1,8,64,128]{3,2,1,0:T(8,128)} %prior_hbm.1, f32[1,8,64,128]{3,2,1,0:T(8,128)} %adj_hbm.1, f32[1,8,64,128]{3,2,1,0:T(8,128)} %after_hbm.1, s32[1]{0:T(128)S(6)} %copy.12.source_any, ...), custom_call_target="tpu_custom_call" | custom-call | tf_op jit(solution)/shard_map/window/pallas_call | solution.py:638
  37.2 0.7 %copy.14 = f32[8,64,128]{2,1,0:T(8,128)} copy(f32[8,64,128]{2,1,0:T(8,128)S(1)} %bitcast.1) | data formatting | bytes 524288
Async XLA Ops:
  0.0 1.3 %copy-start = (f32[1,2,256]{2,1,0:T(2,128)S(1)}, f32[1,2,256]{2,1,0:T(2,128)}, u32[]{:S(2)}) copy-start(f32[1,2,256]{2,1,0:T(2,128)} %traces_any.1) | copy-start | bytes 6148
  0.7 0.7 %copy-start.1 = (s32[1,256]{1,0:T(1,128)S(1)}, s32[1,256]{1,0:T(1,128)}, u32[]{:S(2)}) copy-start(s32[1,256]{1,0:T(1,128)} %cells_any.1) | copy-start | bytes 3076
